TPU v7x, 32 devices: a whole 2x2x4 slice. The times are simulated.
32 devices in a mesh: fsdp: 16 (over z, y, x), ctx: 2 (over core).
Axes of the slice: x: 2, y: 2, z: 4, core: 2. Of those that a mesh axis runs over, the one named last changes fastest.
Arguments:
- tokens: bfloat16 [16, 1024, 768], P('fsdp', 'ctx'), may hold values from -6 to 6
- lengths: int32 [16], P('fsdp'), may hold values from 768 to 1024
- cotangent: bfloat16 [16, 1024, 768], P('fsdp', 'ctx'), may hold values from -6 to 6
- projection: bfloat16 [768, 2304], P('fsdp'), may hold values from -0.3125 to 0.3125
- mixing: bfloat16 [768, 768], P('fsdp'), may hold values from -0.625 to 0.625
- widening: bfloat16 [768, 3072], P('fsdp'), may hold values from -0.21875 to 0.21875
- narrowing: bfloat16 [3072, 768], P('fsdp'), may hold values from -0.15625 to 0.15625
- biases: bfloat16 [4, 768], P(None, 'fsdp'), may hold values from -1.5 to 1.5
- widen_bias: bfloat16 [3072], P('fsdp'), may hold values from -2.5 to 2.5
- norms: bfloat16 [4, 768], P(None, 'fsdp'), may hold values from -1.2 to 1.4, as said below
Outputs:
- result: bfloat16 [16, 1024, 768], P('fsdp', 'ctx')
- grad_tokens: float32 [16, 1024, 768], P('fsdp', 'ctx')
- grad_projection: float32 [768, 2304], P('fsdp')
- grad_mixing: float32 [768, 768], P('fsdp')
- grad_widening: float32 [768, 3072], P('fsdp')
- grad_narrowing: float32 [3072, 768], P('fsdp')
- grad_biases: float32 [4, 768], P(None, 'fsdp')
- grad_widen: float32 [3072], P('fsdp')
- grad_norms: float32 [4, 768], P(None, 'fsdp')
Inputs may be any that keep to these rules, and one draw needn't show every extreme that they name: `norms`: rows 0 and 2 are gains near 1, rows 1 and 3 shifts near 0.
All inputs are finite; a program needn't handle non-finite values.
Results may differ from a plain program's by a relative error of at most 0.014.
The roundings to bfloat16 on the way count: a program that leaves them out, or rounds other values in their place, can miss the bound.
Values may be sent and summed in bfloat16 or wider, within the bound.
No kernel may reach another device: no remote copies, remote signals or barrier semaphores. Data moves between devices by JAX's collectives and lax.ppermute only.
A program may use at most 192 MiB of HBM per device.

v0:
```python
import functools

import jax
import jax.numpy as jnp
from jax import lax
from jax.experimental import pallas as pl
from jax.experimental.pallas import tpu as pltpu
from jax.sharding import PartitionSpec as P

HEADS = 12
HEAD_DIM = 64


EPSILON = 1e-12


def split_heads(matrix):
    return matrix.reshape(matrix.shape[0], HEADS, matrix.shape[1] // HEADS)


def pair_scores(left_rows, right_rows, factor):
    return (
        jnp.einsum(
            "ahd,bhd->hab",
            split_heads(left_rows),
            split_heads(right_rows),
            preferred_element_type=jnp.float32,
        )
        * factor
    )


def spread_rows(weights_hab, right_rows):
    out_rows = jnp.einsum(
        "hab,bhd->ahd", weights_hab, split_heads(right_rows), preferred_element_type=jnp.float32
    )
    return out_rows.reshape(out_rows.shape[0], -1)


def collect_rows(weights_hab, left_rows):
    out_rows = jnp.einsum(
        "hab,ahd->bhd", weights_hab, split_heads(left_rows), preferred_element_type=jnp.float32
    )
    return out_rows.reshape(out_rows.shape[0], -1)


def norm_forward(hidden, gain, shift):
    row_mean = jnp.mean(hidden, axis=-1, keepdims=True)
    centred = hidden - row_mean
    inverse = lax.rsqrt(jnp.mean(centred * centred, axis=-1, keepdims=True) + EPSILON)
    normed = centred * inverse
    return (normed * gain + shift, normed, inverse)


def norm_backward(upstream, normed, inverse, gain):
    inner = upstream * gain
    return inverse * (
        inner
        - jnp.mean(inner, axis=-1, keepdims=True)
        - normed * jnp.mean(inner * normed, axis=-1, keepdims=True)
    )


def gelu_exact(values_in):
    return jax.nn.gelu(values_in, approximate=False)


def general_body(
    tokens, lengths, cotangent, projection, mixing, widening, narrowing, biases, widen_bias, norms
):
    score_scale = HEAD_DIM ** (-0.5)
    gathered = (
        lax.all_gather(projection, "fsdp", axis=0, tiled=True),
        lax.all_gather(mixing, "fsdp", axis=0, tiled=True),
        lax.all_gather(widening, "fsdp", axis=0, tiled=True),
        lax.all_gather(narrowing, "fsdp", axis=0, tiled=True),
        lax.all_gather(biases, "fsdp", axis=1, tiled=True),
        lax.all_gather(widen_bias, "fsdp", axis=0, tiled=True),
        lax.all_gather(norms, "fsdp", axis=1, tiled=True),
    )
    w_project, w_mixing, w_widen, w_narrow, bias_rows, widen_all, norm_rows = gathered
    bias_float = bias_rows.astype(jnp.float32)
    widen_float = widen_all.astype(jnp.float32)
    norm_float = norm_rows.astype(jnp.float32)
    inputs = tokens[0]
    row_count, model_width = inputs.shape
    seq_length = lengths[0]
    joined_rows = jnp.dot(inputs, w_project, preferred_element_type=jnp.float32)
    queries = (joined_rows[:, :model_width] + bias_float[0]).astype(jnp.bfloat16)
    key_rows = joined_rows[:, model_width : 2 * model_width].astype(jnp.bfloat16)
    value_rows = (joined_rows[:, 2 * model_width :] + bias_float[1]).astype(jnp.bfloat16)
    all_keys, all_values = (
        lax.all_gather(key_rows, "ctx", axis=0, tiled=True),
        lax.all_gather(value_rows, "ctx", axis=0, tiled=True),
    )
    key_valid = jnp.arange(all_keys.shape[0], dtype=jnp.int32) < seq_length
    scores = jnp.where(key_valid[None, None, :], pair_scores(queries, all_keys, score_scale), -1e30)
    row_peak = jnp.max(scores, axis=-1, keepdims=True)
    exp_terms = jnp.exp(scores - row_peak)
    summed = jnp.sum(exp_terms, axis=-1, keepdims=True)
    prob_low = (exp_terms / summed).astype(jnp.bfloat16)
    logsum = row_peak + jnp.log(summed)
    mixed_low = spread_rows(prob_low, all_values).astype(jnp.bfloat16)
    branch = jnp.dot(mixed_low, w_mixing, preferred_element_type=jnp.float32) + bias_float[2]
    first_norm, normed_one, inverse_one = norm_forward(
        inputs.astype(jnp.float32) + branch, norm_float[0], norm_float[1]
    )
    first_low = first_norm.astype(jnp.bfloat16)
    expanded = jnp.dot(first_low, w_widen, preferred_element_type=jnp.float32) + widen_float
    activated, gelu_pull = jax.vjp(gelu_exact, expanded)
    active_low = activated.astype(jnp.bfloat16)
    second = jnp.dot(active_low, w_narrow, preferred_element_type=jnp.float32) + bias_float[3]
    result, normed_two, inverse_two = norm_forward(
        first_norm + second, norm_float[2], norm_float[3]
    )
    grad_out = cotangent[0].astype(jnp.float32)
    grad_two = norm_backward(grad_out, normed_two, inverse_two, norm_float[2])
    second_grad = grad_two.astype(jnp.bfloat16)
    narrow_term = jnp.einsum(
        "rf,rd->fd", active_low, second_grad, preferred_element_type=jnp.float32
    )
    active_grad = jnp.einsum("rd,fd->rf", second_grad, w_narrow, preferred_element_type=jnp.float32)
    expand_grad = gelu_pull(active_grad)[0].astype(jnp.bfloat16)
    widen_term = jnp.einsum("rd,rf->df", first_low, expand_grad, preferred_element_type=jnp.float32)
    first_grad = grad_two + jnp.einsum(
        "rf,df->rd", expand_grad, w_widen, preferred_element_type=jnp.float32
    )
    grad_one = norm_backward(first_grad, normed_one, inverse_one, norm_float[0])
    branch_grad = grad_one.astype(jnp.bfloat16)
    mixing_term = jnp.einsum(
        "rd,re->de", mixed_low, branch_grad, preferred_element_type=jnp.float32
    )
    mixed_grad = jnp.einsum(
        "re,de->rd", branch_grad, w_mixing, preferred_element_type=jnp.float32
    ).astype(jnp.bfloat16)
    scores = jnp.where(key_valid[None, None, :], pair_scores(queries, all_keys, score_scale), -1e30)
    prob_again = jnp.exp(scores - logsum)
    prob_grad = pair_scores(mixed_grad, all_values, 1.0)
    row_delta = jnp.sum(prob_again * prob_grad, axis=-1, keepdims=True)
    score_grad = (prob_again * (prob_grad - row_delta)).astype(jnp.bfloat16)
    query_grad = (spread_rows(score_grad, all_keys) * score_scale).astype(jnp.bfloat16)
    key_terms = collect_rows(score_grad, queries) * score_scale
    value_terms = collect_rows(prob_low, mixed_grad)
    key_grad, value_grad = (
        lax.psum_scatter(key_terms, "ctx", scatter_dimension=0, tiled=True),
        lax.psum_scatter(value_terms, "ctx", scatter_dimension=0, tiled=True),
    )
    key_low = key_grad.astype(jnp.bfloat16)
    value_low = value_grad.astype(jnp.bfloat16)
    joined_grad = jnp.concatenate([query_grad, key_low, value_low], axis=1)
    project_term = jnp.einsum("rd,re->de", inputs, joined_grad, preferred_element_type=jnp.float32)
    input_grad = (
        jnp.einsum("re,de->rd", joined_grad, w_project, preferred_element_type=jnp.float32)
        + grad_one
    )
    bias_terms = jnp.stack(
        [
            jnp.sum(query_grad.astype(jnp.float32), axis=0),
            jnp.sum(value_low.astype(jnp.float32), axis=0),
            jnp.sum(branch_grad.astype(jnp.float32), axis=0),
            jnp.sum(second_grad.astype(jnp.float32), axis=0),
        ]
    )
    widen_terms = jnp.sum(expand_grad.astype(jnp.float32), axis=0)
    norm_terms = jnp.stack(
        [
            jnp.sum(first_grad * normed_one, axis=0),
            jnp.sum(first_grad, axis=0),
            jnp.sum(grad_out * normed_two, axis=0),
            jnp.sum(grad_out, axis=0),
        ]
    )
    shares = (
        lax.psum_scatter(project_term, "fsdp", scatter_dimension=0, tiled=True),
        lax.psum_scatter(mixing_term, "fsdp", scatter_dimension=0, tiled=True),
        lax.psum_scatter(widen_term, "fsdp", scatter_dimension=0, tiled=True),
        lax.psum_scatter(narrow_term, "fsdp", scatter_dimension=0, tiled=True),
        lax.psum_scatter(bias_terms, "fsdp", scatter_dimension=1, tiled=True),
        lax.psum_scatter(widen_terms, "fsdp", scatter_dimension=0, tiled=True),
        lax.psum_scatter(norm_terms, "fsdp", scatter_dimension=1, tiled=True),
    )
    totals = lax.psum(
        (shares[0], shares[1], shares[2], shares[3], shares[4], shares[5], shares[6]), "ctx"
    )
    return (
        result.astype(jnp.bfloat16)[None],
        input_grad[None],
        totals[0],
        totals[1],
        totals[2],
        totals[3],
        totals[4],
        totals[5],
        totals[6],
    )


NT=(((1,),(1,)),((),()))
NN=(((1,),(0,)),((),()))
def dotf(a,b,dims): return lax.dot_general(a,b,dims,preferred_element_type=jnp.float32)

def cost(microseconds):
    return pl.CostEstimate(flops=int(microseconds * 5e7), bytes_accessed=2**12, transcendentals=0)


def attn_fwd_kernel(len_ref,q_ref,k_ref,v_ref,*refs):
    o_ref,lse_ref,vt_ref=refs[-3:]
    @pl.when(pl.program_id(1)==0)
    def _():
        vt_ref[...]=v_ref[...].T
    n=len_ref[0]
    q=q_ref[...]; k=k_ref[...]
    lanes=lax.broadcasted_iota(jnp.int32,q.shape,1)
    rows=lax.broadcasted_iota(jnp.int32,(k.shape[0],1),0)
    valid=rows<n
    outs = []
    for h in range(2):
        qh=jnp.where((lanes>=64)==(h==1),q*jnp.bfloat16(HEAD_DIM**-0.5),jnp.bfloat16(0))
        s=dotf(k,qh,NT)
        s=jnp.where(valid,s,-1e30)
        m=jnp.max(s,axis=0,keepdims=True)
        e=jnp.exp(s-m)
        l=jnp.sum(e,axis=0,keepdims=True)
        p=(e*(1.0/l)).astype(jnp.bfloat16)
        lse_ref[0,h:h+1,:]=m+jnp.log(l)
        outs.append(dotf(vt_ref[64*h:64*h+64,:],p,NN))
    o=jnp.concatenate(outs,axis=0)
    o_ref[...]=o.T.astype(jnp.bfloat16)

def attn_fwd(length, joined, before, QB=512):
    L = joined.shape[0]
    C = joined.shape[1] // 3
    pairs = C // 128
    QB = min(QB, L)
    return pl.pallas_call(
        attn_fwd_kernel,
        grid=(pairs, L // QB),
        in_specs=[
            pl.BlockSpec(memory_space=pltpu.SMEM),
            pl.BlockSpec((QB, 128), lambda p, i: (i, p)),
            pl.BlockSpec((L, 128), lambda p, i: (0, pairs + p)),
            pl.BlockSpec((L, 128), lambda p, i: (0, 2 * pairs + p)),
        ]
        + [pl.BlockSpec(memory_space=pl.ANY)] * len(before),
        out_specs=[
            pl.BlockSpec((QB, 128), lambda p, i: (i, p)),
            pl.BlockSpec((1, 2, QB), lambda p, i: (p, 0, i)),
        ],
        out_shape=[
            jax.ShapeDtypeStruct((L, C), jnp.bfloat16),
            jax.ShapeDtypeStruct((pairs, 2, L), jnp.float32),
        ],
        scratch_shapes=[pltpu.VMEM((128, L), jnp.bfloat16)],
        compiler_params=pltpu.CompilerParams(vmem_limit_bytes=20 * 2**20),
        cost_estimate=cost(14.5),
        name="attn_fwd",
    )(length, joined, joined, joined, *before)


def attn_bwd_kernel(core_ref, len_ref, q_ref, k_ref, v_ref, do_ref, do_other_ref, lse_ref, *refs):
    df_ref, sum_ref, kt_ref, dka_ref, dva_ref = refs[-5:]
    i = pl.program_id(1)

    @pl.when(i == 0)
    def _():
        kt_ref[...] = k_ref[...].T
        dka_ref[...] = jnp.zeros_like(dka_ref)
        dva_ref[...] = jnp.zeros_like(dva_ref)

    n = len_ref[0]
    scale = jnp.bfloat16(HEAD_DIM**-0.5)
    q = q_ref[...]
    k = k_ref[...]
    v = v_ref[...]
    do = jnp.where(i == core_ref[0], do_ref[...], do_other_ref[...])
    lanes = lax.broadcasted_iota(jnp.int32, q.shape, 1)
    valid = lax.broadcasted_iota(jnp.int32, (k.shape[0], 1), 0) < n
    outs = []
    for h in range(2):
        mine = (lanes >= HEAD_DIM) == (h == 1)
        qh = jnp.where(mine, q * scale, jnp.bfloat16(0))
        doh = jnp.where(mine, do, jnp.bfloat16(0))
        s = dotf(k, qh, NT)
        p = jnp.where(valid, jnp.exp(s - lse_ref[0, h : h + 1, :]), 0.0)
        dp = dotf(v, doh, NT)
        delta = jnp.sum(p * dp, axis=0, keepdims=True)
        ds = (p * (dp - delta)).astype(jnp.bfloat16)
        dva_ref[...] += dotf(p.astype(jnp.bfloat16), doh, NN)
        dka_ref[...] += dotf(ds, qh, NN)
        outs.append(dotf(kt_ref[HEAD_DIM * h : HEAD_DIM * (h + 1), :], ds, NN))
    dq = jnp.concatenate(outs, axis=0) * (HEAD_DIM**-0.5)
    df_ref[pl.ds(pl.multiple_of(i * q.shape[0], q.shape[0]), q.shape[0]), 0:128] = dq.T.astype(jnp.bfloat16)

    @pl.when(i == pl.num_programs(1) - 1)
    def _():
        df_ref[:, 128:256] = dka_ref[...].astype(jnp.bfloat16)
        df_ref[:, 256:384] = dva_ref[...].astype(jnp.bfloat16)
        sum_ref[0:1, :] = jnp.sum(df_ref[...].astype(jnp.float32), axis=0, keepdims=True)


def attn_bwd(core, length, joined, do, do_other, lse, before):
    L = joined.shape[0]
    pairs = joined.shape[1] // 384
    QB = L // 2
    block = lambda at: pl.BlockSpec((QB, 128), lambda p, i, c: (i, at * pairs + p))
    whole = lambda at: pl.BlockSpec((L, 128), lambda p, i, c: (0, at * pairs + p))
    return pl.pallas_call(
        attn_bwd_kernel,
        grid_spec=pltpu.PrefetchScalarGridSpec(
            num_scalar_prefetch=1,
            grid=(pairs, 2),
            in_specs=[
                pl.BlockSpec(memory_space=pltpu.SMEM),
                block(0),
                whole(1),
                whole(2),
                pl.BlockSpec((QB, 128), lambda p, i, c: (0, c[0] * pairs + p)),
                pl.BlockSpec((QB, 128), lambda p, i, c: (0, p)),
                pl.BlockSpec((1, 2, QB), lambda p, i, c: (p, 0, i)),
            ]
            + [pl.BlockSpec(memory_space=pl.ANY)] * len(before),
            out_specs=[
                pl.BlockSpec((L, 384), lambda p, i, c: (0, p)),
                pl.BlockSpec((8, 384), lambda p, i, c: (0, p)),
            ],
            scratch_shapes=[
                pltpu.VMEM((128, L), jnp.bfloat16),
                pltpu.VMEM((L, 128), jnp.float32),
                pltpu.VMEM((L, 128), jnp.float32),
            ],
        ),
        out_shape=[
            jax.ShapeDtypeStruct((L, pairs * 384), jnp.bfloat16),
            jax.ShapeDtypeStruct((8, pairs * 384), jnp.float32),
        ],
        compiler_params=pltpu.CompilerParams(vmem_limit_bytes=20 * 2**20),
        cost_estimate=cost(22.0),
        name="attn_bwd",
    )(core, length, joined, joined, joined, do, do_other, lse, *before)


TN = (((0,), (0,)), ((), ()))


def gelu_pair(z):
    cdf = 0.5 * (1.0 + lax.erf(z * (0.5**0.5)))
    pdf = jnp.exp(-0.5 * z * z) * ((0.5 / jnp.pi) ** 0.5)
    return z * cdf, cdf + z * pdf

def widen_kernel(core_ref, own_ref, other_ref, mix_own_ref, mix_other_ref, x_ref, rows_ref, w_ref, wb_ref,
                 low_ref, turned_ref, normed_ref, inverse_ref, g_ref, gp_ref, z_ref):
    @pl.when(pl.program_id(0) == 0)
    def _():
        width = x_ref.shape[1]
        branch = dotf(own_ref[...], mix_own_ref[...].reshape(width // 2, width), NN)
        branch += dotf(other_ref[...], mix_other_ref[...].reshape(width // 2, width), NN)
        hidden = x_ref[...].astype(jnp.float32) + (branch + rows_ref[2:3, :])
        centred = hidden - jnp.mean(hidden, axis=1, keepdims=True)
        inverse = lax.rsqrt(jnp.mean(centred * centred, axis=1, keepdims=True) + EPSILON)
        normed = centred * inverse
        normed_ref[...] = normed
        inverse_ref[...] = inverse
        low_ref[...] = (normed * rows_ref[4:5, :] + rows_ref[5:6, :]).astype(jnp.bfloat16)
        turned_ref[...] = low_ref[...].T

    widen_block(low_ref, w_ref, wb_ref, g_ref, gp_ref, z_ref)


def widen_block(low_ref, w_ref, wb_ref, g_ref, gp_ref, z_ref):
    rows = 64
    z_ref[...] = dotf(low_ref[...], w_ref[...].reshape(low_ref.shape[1], -1), NN)

    def step(i, carry):
        at = pl.ds(i * rows, rows)
        value, slope = gelu_pair(z_ref[at, :] + wb_ref[...])
        g_ref[at, :] = value.astype(jnp.bfloat16)
        gp_ref[at, :] = slope
        return carry

    lax.fori_loop(0, z_ref.shape[0] // rows, step, 0)


def widen(core, mixed_own, mixed_other, rest, narrow_rows, inputs, rows_float, widen_bias):
    rows, width = inputs.shape
    chips = rest.shape[0]
    shard = width // chips
    blocks = widen_bias.shape[1] // width
    half = width // 2
    start = narrow_rows // shard
    fixed = lambda shape: pl.BlockSpec(shape, lambda j, c: (0,) * len(shape))
    return pl.pallas_call(
        widen_kernel,
        grid_spec=pltpu.PrefetchScalarGridSpec(
            num_scalar_prefetch=1,
            grid=(blocks,),
            in_specs=[
                pl.BlockSpec((rows, half), lambda j, c: (c[0], 0)),
                pl.BlockSpec((rows, half), lambda j, c: (c[0], 0)),
                pl.BlockSpec((chips // 2, shard, width), lambda j, c: (c[0], start, 0)),
                pl.BlockSpec((chips // 2, shard, width), lambda j, c: (1 - c[0], start, 0)),
                fixed((rows, width)),
                fixed(rows_float.shape),
                pl.BlockSpec((chips, shard, width), lambda j, c: (0, start + 1 + j, 0)),
                pl.BlockSpec((1, width), lambda j, c: (0, j)),
            ],
            out_specs=[
                fixed((rows, width)),
                fixed((width, rows)),
                fixed((rows, width)),
                fixed((rows, 1)),
                pl.BlockSpec((rows, width), lambda j, c: (0, j)),
                pl.BlockSpec((rows, width), lambda j, c: (0, j)),
            ],
            scratch_shapes=[pltpu.VMEM((rows, width), jnp.float32)],
        ),
        out_shape=[
            jax.ShapeDtypeStruct((rows, width), jnp.bfloat16),
            jax.ShapeDtypeStruct((width, rows), jnp.bfloat16),
            jax.ShapeDtypeStruct((rows, width), jnp.float32),
            jax.ShapeDtypeStruct((rows, 1), jnp.float32),
            jax.ShapeDtypeStruct((rows, blocks * width), jnp.bfloat16),
            jax.ShapeDtypeStruct((rows, blocks * width), jnp.float32),
        ],
        compiler_params=pltpu.CompilerParams(vmem_limit_bytes=20 * 2**20),
        cost_estimate=cost(12.5),
        name="widen",
    )(core, mixed_own, mixed_other, rest, rest, inputs, rows_float, rest, widen_bias)


def back_kernel(core_ref, dm_ref, grad_two_ref, normed_ref, inverse_ref, rows_ref, narrow_ref, w_ref, gp_ref,
                mix_ref, *refs, spare):
    (dz_own_ref, dz_other_ref, columns_ref, one_ref, da_ref, da_other_ref, do_ref, do_other_ref, sums_ref,
     acc_ref) = refs[spare:]
    j = pl.program_id(0)
    rows, width = dm_ref.shape
    half = width // 2
    at_other = pl.ds(pl.multiple_of((1 - core_ref[0]) * half, half), half)
    dz = dotf(dm_ref[...], narrow_ref[...].reshape(width, width), NT) * gp_ref[...]
    dz = dz.astype(jnp.bfloat16)
    own_turn = j >= pl.num_programs(0) // 2

    @pl.when(own_turn)
    def _():
        dz_own_ref[...] = dz

    @pl.when(jnp.logical_not(own_turn))
    def _():
        dz_other_ref[...] = dz

    sums = jnp.broadcast_to(jnp.sum(dz.astype(jnp.float32), axis=0, keepdims=True), (128, width)).T
    shard = mix_ref.shape[1]
    chips = columns_ref.shape[0] // shard
    each = width // chips // shard
    lanes = lax.broadcasted_iota(jnp.int32, (shard, 128), 1)
    for chip in range(chips):
        total = jnp.zeros((shard, 128), jnp.float32)
        for k in range(each):
            at = (chip * each + k) * shard
            total = jnp.where(lanes == 8 + k, sums[at : at + shard, :], total)
        columns_ref[chip * shard : (chip + 1) * shard, :] = total
    part = dotf(dz, w_ref[...].reshape(width, -1), NT)

    @pl.when(j == 0)
    def _():
        acc_ref[...] = grad_two_ref[...] + part

    @pl.when(j > 0)
    def _():
        acc_ref[...] += part

    @pl.when(j == pl.num_programs(0) - 1)
    def _():
        first_grad = acc_ref[...]
        normed = normed_ref[...]
        inner = first_grad * rows_ref[4:5, :]
        one = inverse_ref[...] * (
            inner
            - jnp.mean(inner, axis=1, keepdims=True)
            - normed * jnp.mean(inner * normed, axis=1, keepdims=True)
        )
        one_ref[...] = one
        low = one.astype(jnp.bfloat16)
        da_ref[...] = low
        da_other_ref[...] = da_ref[:, at_other]
        do_ref[...] = dotf(low, mix_ref[...].reshape(width, width), NT).astype(jnp.bfloat16)
        do_other_ref[...] = do_ref[:, at_other]
        sums_ref[0:1, :] = jnp.sum(first_grad * normed, axis=0, keepdims=True)
        sums_ref[1:2, :] = jnp.sum(first_grad, axis=0, keepdims=True)
        sums_ref[2:3, :] = jnp.sum(low.astype(jnp.float32), axis=0, keepdims=True)


def back(core, dm, grad_two, normed, inverse, rows_float, rest, narrow_rows, gp, chips, before):
    rows, width = dm.shape
    shard = width // chips
    half = width // 2
    blocks = gp.shape[1] // width
    start = narrow_rows // shard
    at = lambda j, c: (j + (1 - c[0]) * (blocks // 2)) % blocks
    fixed = lambda shape: pl.BlockSpec(shape, lambda j, c: (0,) * len(shape))
    low = lambda shape: jax.ShapeDtypeStruct(shape, jnp.bfloat16)
    return pl.pallas_call(
        functools.partial(back_kernel, spare=len(before)),
        grid_spec=pltpu.PrefetchScalarGridSpec(
            num_scalar_prefetch=1,
            grid=(blocks,),
            in_specs=[
                fixed((rows, width)),
                fixed((rows, width)),
                fixed((rows, width)),
                fixed((rows, 1)),
                fixed(rows_float.shape),
                pl.BlockSpec((width // narrow_rows, narrow_rows, width), lambda j, c: (at(j, c), 0, 0)),
                pl.BlockSpec((chips, shard, width), lambda j, c: (0, start + 1 + at(j, c), 0)),
                pl.BlockSpec((rows, width), lambda j, c: (0, at(j, c))),
                pl.BlockSpec((chips, shard, width), lambda j, c: (0, start, 0)),
            ]
            + [pl.BlockSpec(memory_space=pl.ANY)] * len(before),
            out_specs=[
                pl.BlockSpec((rows, width), lambda j, c: (0, jnp.maximum(j - blocks // 2, 0))),
                pl.BlockSpec((rows, width), lambda j, c: (0, jnp.minimum(j, blocks // 2 - 1))),
                pl.BlockSpec((width // blocks, 128), lambda j, c: (at(j, c), 0)),
                fixed((rows, width)),
                fixed((rows, width)),
                fixed((rows, half)),
                fixed((rows, width)),
                fixed((rows, half)),
                fixed((8, width)),
            ],
            scratch_shapes=[pltpu.VMEM((rows, width), jnp.float32)],
        ),
        out_shape=[
            low((rows, blocks // 2 * width)),
            low((rows, blocks // 2 * width)),
            jax.ShapeDtypeStruct((width, 128), jnp.float32),
            jax.ShapeDtypeStruct((rows, width), jnp.float32),
            low((rows, width)),
            low((rows, half)),
            low((rows, width)),
            low((rows, half)),
            jax.ShapeDtypeStruct((8, width), jnp.float32),
        ],
        compiler_params=pltpu.CompilerParams(vmem_limit_bytes=56 * 2**20),
        cost_estimate=cost(13.8),
        name="back",
    )(core, dm, grad_two, normed, inverse, rows_float, rest, rest, gp, rest, *before)


def tokens_kernel(core_ref, grad_ref, w_ref, one_ref, *refs):
    own_ref, other_ref = refs[-2:]
    half = w_ref.shape[1] // 3

    def part():
        total = 0.0
        for pair in range(half // 128):
            for kind in range(3):
                at = kind * half + pair * 128
                start = pair * 384 + kind * 128
                total += dotf(grad_ref[:, start : start + 128], w_ref[:, at : at + 128], NT)
        return total

    @pl.when(pl.program_id(0) == 0)
    def _():
        other_ref[...] = part()

    @pl.when(pl.program_id(0) == 1)
    def _():
        own_ref[...] = part() + one_ref[...]


def tokens_grad(core, grad, w_own, grad_one, before):
    rows, width = grad_one.shape
    fixed = lambda shape: pl.BlockSpec(shape, lambda i, c: (0,) * len(shape))
    return pl.pallas_call(
        tokens_kernel,
        grid_spec=pltpu.PrefetchScalarGridSpec(
            num_scalar_prefetch=1,
            grid=(2,),
            in_specs=[
                pl.BlockSpec((rows, grad.shape[1]), lambda i, c: (jnp.where(i == 0, 1 - c[0], c[0]), 0)),
                fixed(w_own.shape),
                fixed((rows, width)),
            ]
            + [pl.BlockSpec(memory_space=pl.ANY)] * len(before),
            out_specs=[fixed((rows, width)), fixed((rows, width))],
        ),
        out_shape=[jax.ShapeDtypeStruct((rows, width), jnp.float32)] * 2,
        compiler_params=pltpu.CompilerParams(vmem_limit_bytes=20 * 2**20),
        cost_estimate=cost(100.0),
        name="tokens_grad",
    )(core, grad, w_own, grad_one, *before)


def widen_grad_kernel(own_ref, other_ref, grad_own_ref, grad_other_ref, left_ref, right_ref):
    term = dotf(own_ref[...], grad_own_ref[...], NN) + dotf(other_ref[...], grad_other_ref[...], NN)

    @pl.when(pl.program_id(0) == 0)
    def _():
        left_ref[...] = term.astype(jnp.bfloat16)

    @pl.when(pl.program_id(0) == 1)
    def _():
        right_ref[...] = term.astype(jnp.bfloat16)


def widen_grad(turned, turned_other, grad, grad_other):
    width, rows = turned.shape
    columns = grad.shape[1] // 2
    fixed = lambda shape: pl.BlockSpec(shape, lambda i: (0, 0))
    return pl.pallas_call(
        widen_grad_kernel,
        grid=(2,),
        in_specs=[fixed((width, rows))] * 2 + [pl.BlockSpec((rows, columns), lambda i: (0, i))] * 2,
        out_specs=[fixed((width, columns))] * 2,
        out_shape=[jax.ShapeDtypeStruct((width, columns), jnp.bfloat16)] * 2,
        compiler_params=pltpu.CompilerParams(vmem_limit_bytes=16 * 2**20),
        cost_estimate=cost(4.0),
        name="widen_grad",
    )(turned, turned_other, grad, grad_other)


def last_grad_kernel(core_ref, turned_ref, grad_ref, mixing_ref, grad_sums_ref, first_ref, second_ref, widen_ref,
                     left_ref, right_ref):
    half = mixing_ref.shape[1]
    pairs = grad_ref.shape[1] // 384
    left_ref[:, :half] = mixing_ref[...]
    for pair in range(pairs):
        term = dotf(turned_ref[...], grad_ref[:, pair * 384 : pair * 384 + 384], NN).astype(jnp.bfloat16)
        if pair == 0:
            left_ref[:, half:] = term
        else:
            right_ref[:, pair * 384 - 384 : pair * 384] = term

    def columns(rows):
        place = lax.broadcasted_iota(jnp.int32, (128, rows[0][1].shape[1]), 0)
        total = 0.0
        for at, row in rows:
            total = jnp.where(place == at, row, total)
        return total.T

    small = pl.ds(pairs * 384 - 384, 128)
    given = [(2, first_ref[2:3, :]), (3, second_ref[0:1, :]), (4, first_ref[0:1, :])]
    given += [(5, first_ref[1:2, :]), (6, second_ref[1:2, :]), (7, second_ref[2:3, :])]
    right_ref[:, small] = (columns(given) + widen_ref[...]).astype(jnp.bfloat16)
    sums = grad_sums_ref[0:1, :]
    queries = jnp.concatenate([sums[:, pair * 384 : pair * 384 + 128] for pair in range(pairs)], axis=1)
    values = jnp.concatenate([sums[:, pair * 384 + 256 : pair * 384 + 384] for pair in range(pairs)], axis=1)
    at = pl.ds(pl.multiple_of(core_ref[0] * half, half), half)
    right_ref[at, small] = right_ref[at, small] + columns([(0, queries), (1, values)]).astype(jnp.bfloat16)


def last_grad(core, turned, grad, mixing_term, grad_sums, first_sums, second_sums, widen_columns):
    width = turned.shape[0]
    columns = grad.shape[1]
    whole = pl.BlockSpec(memory_space=pltpu.VMEM)
    return pl.pallas_call(
        last_grad_kernel,
        in_specs=[pl.BlockSpec(memory_space=pltpu.SMEM)] + [whole] * 7,
        out_specs=[whole] * 2,
        out_shape=[
            jax.ShapeDtypeStruct((width, width // 2 + 384), jnp.bfloat16),
            jax.ShapeDtypeStruct((width, columns - 384 + 128), jnp.bfloat16),
        ],
        compiler_params=pltpu.CompilerParams(vmem_limit_bytes=16 * 2**20),
        cost_estimate=cost(4.0),
        name="last_grad",
    )(core, turned, grad, mixing_term, grad_sums, first_sums, second_sums, widen_columns)


def finish_kernel(core_ref, own_ref, other_ref, *refs, half):
    project_ref, mixing_ref, small_ref = refs[-3:]
    for ref, core in ((own_ref, core_ref[0]), (other_ref, 1 - core_ref[0])):
        mixing_ref[:, pl.ds(pl.multiple_of(core * half, half), half)] = ref[:, :half]
        for pair in range(half // 128):
            for kind in range(3):
                start = half + pair * 384 + kind * 128
                to = pl.multiple_of(core * half + (kind * 2 * half + pair * 128), 128)
                project_ref[:, pl.ds(to, 128)] = ref[:, start : start + 128]
    small = own_ref[:, 4 * half :] + other_ref[:, 4 * half :]
    small_ref[...] = small.T


def finish(core, share, other, half, before):
    rows = share.shape[0]
    whole = pl.BlockSpec(memory_space=pltpu.VMEM)
    return pl.pallas_call(
        functools.partial(finish_kernel, half=half),
        in_specs=[pl.BlockSpec(memory_space=pltpu.SMEM)] + [whole] * 2 + [pl.BlockSpec(memory_space=pl.ANY)] * len(before),
        out_specs=[whole] * 3,
        out_shape=[
            jax.ShapeDtypeStruct((rows, 6 * half), jnp.float32),
            jax.ShapeDtypeStruct((rows, 2 * half), jnp.float32),
            jax.ShapeDtypeStruct((128, rows), jnp.float32),
        ],
        compiler_params=pltpu.CompilerParams(vmem_limit_bytes=8 * 2**20),
        cost_estimate=cost(2.0),
        name="finish",
    )(core, share, other, *before)


def narrow_kernel(core_ref, g_ref, w_ref, normed_ref, rows_ref, cot_ref,
                  result_ref, two_ref, dm_ref, dm_own_ref, dm_other_ref, sums_ref, acc_ref):
    j = pl.program_id(0)
    width = w_ref.shape[2]
    half = width // 2
    at_own = pl.ds(pl.multiple_of(core_ref[0] * half, half), half)
    at_other = pl.ds(pl.multiple_of((1 - core_ref[0]) * half, half), half)

    @pl.when(j == 0)
    def _():
        acc_ref[...] = jnp.zeros_like(acc_ref)

    acc_ref[...] += dotf(g_ref[...], w_ref[...].reshape(width, width), NN)

    @pl.when(j == pl.num_programs(0) - 1)
    def _():
        hidden = normed_ref[...] * rows_ref[4:5, :] + rows_ref[5:6, :] + (acc_ref[...] + rows_ref[3:4, :])
        centred = hidden - jnp.mean(hidden, axis=1, keepdims=True)
        inverse = lax.rsqrt(jnp.mean(centred * centred, axis=1, keepdims=True) + EPSILON)
        normed = centred * inverse
        result_ref[...] = (normed * rows_ref[6:7, :] + rows_ref[7:8, :]).astype(jnp.bfloat16)
        cot = cot_ref[...].astype(jnp.float32)
        inner = cot * rows_ref[6:7, :]
        two = inverse * (
            inner
            - jnp.mean(inner, axis=1, keepdims=True)
            - normed * jnp.mean(inner * normed, axis=1, keepdims=True)
        )
        two_ref[...] = two
        dm = two.astype(jnp.bfloat16)
        dm_ref[...] = dm
        dm_own_ref[...] = dm_ref[:, at_own]
        dm_other_ref[...] = dm_ref[:, at_other]
        sums_ref[0:1, :] = jnp.sum(dm.astype(jnp.float32), axis=0, keepdims=True)
        sums_ref[1:2, :] = jnp.sum(cot * normed, axis=0, keepdims=True)
        sums_ref[2:3, :] = jnp.sum(cot, axis=0, keepdims=True)


def narrow(core, g, rest, narrow_rows, normed, rows_float, cotangent):
    rows, width = normed.shape
    half = width // 2
    fixed = lambda shape: pl.BlockSpec(shape, lambda j, c: (0,) * len(shape))
    return pl.pallas_call(
        narrow_kernel,
        grid_spec=pltpu.PrefetchScalarGridSpec(
            num_scalar_prefetch=1,
            grid=(g.shape[1] // width,),
            in_specs=[
                pl.BlockSpec((rows, width), lambda j, c: (0, j)),
                pl.BlockSpec((width // narrow_rows, narrow_rows, width), lambda j, c: (j, 0, 0)),
                fixed((rows, width)),
                fixed(rows_float.shape),
                fixed((rows, width)),
            ],
            out_specs=[
                fixed((rows, width)),
                fixed((rows, width)),
                fixed((rows, width)),
                fixed((rows, half)),
                fixed((rows, half)),
                fixed((8, width)),
            ],
            scratch_shapes=[pltpu.VMEM((rows, width), jnp.float32)],
        ),
        out_shape=[
            jax.ShapeDtypeStruct((rows, width), jnp.bfloat16),
            jax.ShapeDtypeStruct((rows, width), jnp.float32),
            jax.ShapeDtypeStruct((rows, width), jnp.bfloat16),
            jax.ShapeDtypeStruct((rows, half), jnp.bfloat16),
            jax.ShapeDtypeStruct((rows, half), jnp.bfloat16),
            jax.ShapeDtypeStruct((8, width), jnp.float32),
        ],
        compiler_params=pltpu.CompilerParams(vmem_limit_bytes=20 * 2**20),
        cost_estimate=cost(8.0),
        name="narrow",
    )(core, g, rest, normed, rows_float, cotangent)


def narrow_grad_kernel(own_ref, other_ref, dm_own_ref, dm_other_ref, out_ref):
    term = dotf(own_ref[...], dm_own_ref[...], TN) + dotf(other_ref[...], dm_other_ref[...], TN)
    out_ref[...] = term.reshape(out_ref.shape).astype(jnp.bfloat16)


def narrow_grad(g, g_other, dm_own, dm_other, chips):
    rows, hidden = g.shape
    half = dm_own.shape[1]
    lines = chips // 4
    size = hidden // lines
    fixed = lambda shape: pl.BlockSpec(shape, lambda j: (0, 0))
    return pl.pallas_call(
        narrow_grad_kernel,
        grid=(lines,),
        in_specs=[pl.BlockSpec((rows, size), lambda j: (0, j))] * 2 + [fixed((rows, half))] * 2,
        out_specs=pl.BlockSpec((4, 1, size // 4, half), lambda j: (0, j, 0, 0)),
        out_shape=jax.ShapeDtypeStruct((4, lines, size // 4, half), jnp.bfloat16),
        compiler_params=pltpu.CompilerParams(vmem_limit_bytes=12 * 2**20),
        cost_estimate=cost(4.5),
        name="narrow_grad",
    )(g, g_other, dm_own, dm_other)


def mixing_grad_kernel(core_ref, own_ref, other_ref, grad_ref, grad_other_ref, *refs):
    out_ref = refs[-1]
    rows, half = grad_other_ref.shape
    core = core_ref[0]
    here = pl.ds(pl.multiple_of(core * rows, rows), rows)
    there = pl.ds(pl.multiple_of((1 - core) * rows, rows), rows)
    at_own = pl.ds(pl.multiple_of(core * half, half), half)
    at_other = pl.ds(pl.multiple_of((1 - core) * half, half), half)
    grad = grad_ref[:, at_own]
    grad_other = grad_other_ref[...]
    for ref, at in ((own_ref, at_own), (other_ref, at_other)):
        term = dotf(ref[here, :], grad, TN) + dotf(ref[there, :], grad_other, TN)
        out_ref[at, :] = term.astype(jnp.bfloat16)


def mixing_grad(core, mixed_own, mixed_other, grad, grad_other):
    width = grad.shape[1]
    whole = pl.BlockSpec(memory_space=pltpu.VMEM)
    return pl.pallas_call(
        mixing_grad_kernel,
        in_specs=[pl.BlockSpec(memory_space=pltpu.SMEM)] + [whole] * 4,
        out_specs=whole,
        out_shape=jax.ShapeDtypeStruct((width, width // 2), jnp.bfloat16),
        compiler_params=pltpu.CompilerParams(vmem_limit_bytes=12 * 2**20),
        cost_estimate=cost(2.0),
        name="mixing_grad",
    )(core, mixed_own, mixed_other, grad, grad_other)


def qkv_kernel(place_ref, x_ref, left_ref, left_other_ref, right_ref, right_other_ref, joined_ref, w_ref, rows_ref,
               small_ref, *, small_at, far):
    core = place_ref[0]
    y = place_ref[far + 1]
    x = place_ref[far + 2]
    shard, cut = left_ref.shape[-2:]
    lines = left_ref.shape[0]
    for line in range(lines):
        for ref, bit in ((left_ref, y), (left_other_ref, 1 - y)):
            to = pl.multiple_of((line * 4 + bit * 2) * shard, 2 * shard)
            w_ref[pl.ds(to, 2 * shard), :cut] = ref[line].reshape(2 * shard, cut)
        for ref, bit in ((right_ref, x), (right_other_ref, 1 - x)):
            for row in range(2):
                to = pl.multiple_of((line * 4 + row * 2 + bit) * shard, shard)
                w_ref[pl.ds(to, shard), cut:] = ref[line, row, :, :small_at]
                small_ref[pl.ds(to, shard), :] = ref[line, row, :, small_at:].astype(jnp.float32)
    rows_ref[...] = small_ref[...].T[: rows_ref.shape[0]]
    half = w_ref.shape[1] // 3
    at = pl.ds(pl.multiple_of(core * half, half), half)
    product = dotf(x_ref[...], w_ref[...], NN)
    joined_ref[:, :half] = (product[:, :half] + rows_ref[0:1, at]).astype(jnp.bfloat16)
    joined_ref[:, half : 2 * half] = product[:, half : 2 * half].astype(jnp.bfloat16)
    joined_ref[:, 2 * half :] = (product[:, 2 * half :] + rows_ref[1:2, at]).astype(jnp.bfloat16)


def qkv(place, inputs, left, left_other, right, right_other, small_at):
    shard, cut = left.shape[-2:]
    length, width = inputs.shape
    far = left.ndim - 4
    lines = 2**far
    left, left_other = left.reshape(lines, 2, shard, cut), left_other.reshape(lines, 2, shard, cut)
    right, right_other = right.reshape(lines, 2, shard, cut), right_other.reshape(lines, 2, shard, cut)
    whole = pl.BlockSpec(memory_space=pltpu.VMEM)
    return pl.pallas_call(
        functools.partial(qkv_kernel, small_at=small_at, far=far),
        in_specs=[pl.BlockSpec(memory_space=pltpu.SMEM)] + [whole] * 5,
        out_specs=[whole] * 3,
        out_shape=[
            jax.ShapeDtypeStruct((length, cut + small_at), jnp.bfloat16),
            jax.ShapeDtypeStruct((width, cut + small_at), jnp.bfloat16),
            jax.ShapeDtypeStruct((16, width), jnp.float32),
        ],
        scratch_shapes=[pltpu.VMEM((width, 128), jnp.float32)],
        compiler_params=pltpu.CompilerParams(vmem_limit_bytes=56 * 2**20),
        cost_estimate=cost(4.0),
        name="qkv",
    )(place, inputs, left, left_other, right, right_other)


def pack_kernel(core_ref, narrow_ref, mixing_ref, widen_ref, project_ref, biases_ref, norms_ref, hidden_ref,
                rest_ref, packed_ref):
    core = core_ref[0]
    shard, width = mixing_ref.shape
    half = width // 2
    split = rest_ref.shape[0] - narrow_ref.shape[0]
    blocks = widen_ref.shape[1] // width

    @pl.when(core == 0)
    def _():
        rest_ref[: narrow_ref.shape[0]] = narrow_ref[...]
        rest_ref[narrow_ref.shape[0] :] = mixing_ref[:split]

    @pl.when(core == 1)
    def _():
        rest_ref[: shard - split] = mixing_ref[split:]
        for block in range(blocks):
            at = shard - split + block * shard
            rest_ref[at : at + shard] = widen_ref[:, block * width : (block + 1) * width]
        at = shard - split + blocks * shard
        if at < rest_ref.shape[0]:
            rest_ref[at:] = jnp.zeros((rest_ref.shape[0] - at, width), jnp.bfloat16)

    for kind in range(3):
        from_ = pl.ds(pl.multiple_of(core * half + kind * width, half), half)
        packed_ref[:, kind * half : (kind + 1) * half] = project_ref[:, from_]
    place = lax.broadcasted_iota(jnp.int32, (128, shard), 0)
    total = jnp.zeros((128, shard), jnp.float32)
    at = 0
    for ref in (biases_ref, norms_ref, hidden_ref):
        for row in range(ref.shape[0]):
            total = jnp.where(place == at, ref[row : row + 1, :].astype(jnp.float32), total)
            at += 1
    packed_ref[:, 3 * half :] = total.T.astype(jnp.bfloat16)


def pack(core, narrowing, mixing, widening, projection, biases, norms, hidden):
    shard, width = mixing.shape
    rows = narrowing.shape[0] + shard + widening.shape[1] // width * shard
    half_rows = -(-rows // 32) * 16
    whole = pl.BlockSpec(memory_space=pltpu.VMEM)
    return pl.pallas_call(
        pack_kernel,
        in_specs=[pl.BlockSpec(memory_space=pltpu.SMEM)] + [whole] * 7,
        out_specs=[whole] * 2,
        out_shape=[
            jax.ShapeDtypeStruct((half_rows, width), jnp.bfloat16),
            jax.ShapeDtypeStruct((shard, projection.shape[1] // 2 + 128), jnp.bfloat16),
        ],
        compiler_params=pltpu.CompilerParams(vmem_limit_bytes=60 * 2**20),
        cost_estimate=cost(2.0),
        name="pack",
    )(core, narrowing, mixing, widening, projection, biases, norms, hidden)


AXES = ("fsdp", "ctx")


def core_permute(value, chips):
    pairs = [(2 * f + c, 2 * f + 1 - c) for f in range(chips) for c in range(2)]
    return lax.ppermute(value, AXES, pairs)


def chip_permute(value, chips, mask):
    pairs = [(2 * f + c, 2 * (f ^ mask) + c) for f in range(chips) for c in range(2)]
    return lax.ppermute(value, AXES, pairs)


def chip_bit(mask):
    return (lax.axis_index("fsdp") // mask) % 2


def by_core(mine, other, axis):
    core = lax.axis_index("ctx")
    first = jnp.where(core == 0, mine, other)
    second = jnp.where(core == 0, other, mine)
    return jnp.concatenate([first, second], axis=axis)


def dims_of(chips):
    return [1 << b for b in reversed(range(chips.bit_length() - 1))]


def gather_step(value, chips, mask):
    axis = dims_of(chips).index(mask)
    other = chip_permute(value, chips, mask)
    bit = chip_bit(mask)
    first = jnp.where(bit == 0, value, other)
    second = jnp.where(bit == 0, other, value)
    return jnp.concatenate([first, second], axis=axis)


def bits_of(chips):
    return jnp.stack([chip_bit(mask) for mask in dims_of(chips)])


def first_send(value, chips, mask):
    shape = [chips // (2 * mask), 2, mask] + list(value.shape[1:])
    send = lax.dynamic_index_in_dim(value.reshape(shape), 1 - chip_bit(mask), 1, keepdims=False)
    return send.reshape(chips // 2, *value.shape[1:])


def block_at(step, left, free, fixed):
    index = 0
    for place, mask in enumerate(left):
        if mask in fixed:
            bit = fixed[mask]
        else:
            bit = (step // 2 ** (len(free) - 1 - free.index(mask))) % 2
        index = index + bit * 2 ** (len(left) - 1 - place)
    return index


def hop_kernel(bits_ref, *refs, parts, merged, spare):
    outs = refs[4 * parts + spare :]
    at = 0
    for part in range(parts):
        away, away_in, keep, keep_in = refs[4 * part : 4 * part + 4]
        columns = away.shape[2]
        send_ref, keep_ref = outs[:2] if merged else outs[2 * part : 2 * part + 2]
        where = pl.ds(at, columns)
        send_ref[:, :, where] = (away[...].astype(jnp.float32) + away_in[...].astype(jnp.float32)).astype(jnp.bfloat16)
        keep_ref[:, :, where] = keep[...].astype(jnp.float32) + keep_in[...].astype(jnp.float32)
        if merged:
            at += columns


def hop(parts, bits, chips, before, merged):
    masks = dims_of(chips)
    in_specs, operands, out_columns = [], [], []
    steps = 2 ** (len([mask for mask in parts[0][2] if mask != parts[0][3]]) - 1)
    for value, arrived, left, came, goes in parts:
        rows, columns = value.shape[1:]
        rest = [mask for mask in left if mask != came]
        free = [mask for mask in rest if mask != goes]
        block = (1, rows, columns)
        for flip in (1, 0):
            def at_value(i, b, left=left, free=free, came=came, goes=goes, flip=flip):
                mine = b[masks.index(goes)]
                side = 1 - mine if flip else mine
                return block_at(i, left, free, {came: b[masks.index(came)], goes: side}), 0, 0

            def at_arrived(i, b, rest=rest, free=free, goes=goes, flip=flip):
                mine = b[masks.index(goes)]
                return block_at(i, rest, free, {goes: 1 - mine if flip else mine}), 0, 0

            in_specs += [pl.BlockSpec(block, at_value), pl.BlockSpec(block, at_arrived)]
            operands += [value, arrived]
        out_columns.append(columns)
    if merged:
        out_columns = [sum(out_columns)]
    out_specs, out_shape = [], []
    for columns in out_columns:
        out_specs += [pl.BlockSpec((1, rows, columns), lambda i, b: (i, 0, 0))] * 2
        out_shape += [
            jax.ShapeDtypeStruct((steps, rows, columns), jnp.bfloat16),
            jax.ShapeDtypeStruct((steps, rows, columns), jnp.float32),
        ]
    outs = pl.pallas_call(
        functools.partial(hop_kernel, parts=len(parts), merged=merged, spare=len(before)),
        grid_spec=pltpu.PrefetchScalarGridSpec(
            num_scalar_prefetch=1,
            grid=(steps,),
            in_specs=in_specs + [pl.BlockSpec(memory_space=pl.ANY)] * len(before),
            out_specs=out_specs,
        ),
        out_shape=out_shape,
        compiler_params=pltpu.CompilerParams(vmem_limit_bytes=8 * 2**20),
        cost_estimate=cost(2.0),
        name="hop",
    )(bits, *operands, *before)
    return list(outs[0::2]), list(outs[1::2])


class Chain:
    def __init__(self, values, chips, bits):
        self.chips, self.bits, self.masks = chips, bits, dims_of(chips)
        self.far = self.masks[:-2]
        self.order = ([1, 2], [2, 1])
        self.kept = values
        self.sent = [first_send(part, chips, order[0]) for part, order in zip(self.kept, self.order)]

    def move(self, masks):
        self.arrived = [chip_permute(part, self.chips, mask) for part, mask in zip(self.sent, masks)]

    def first(self):
        self.move([1, 2])

    def second(self, before):
        self.sent, self.kept = hop(
            [
                (kept, arrived, self.masks, order[0], order[1])
                for kept, arrived, order in zip(self.kept, self.arrived, self.order)
            ],
            self.bits, self.chips, before, False,
        )
        self.move([2, 1])

    def third(self, before, others=()):
        parts = [
            (kept, arrived, self.far, order[1], self.far[-1])
            for chain in (self, *others)
            for kept, arrived, order in zip(chain.kept, chain.arrived, chain.order)
        ]
        self.sent, self.kept = hop(parts, self.bits, self.chips, before, True)
        self.move([self.far[-1]])

    def fourth(self, before):
        for at in range(len(self.far) - 1, 0, -1):
            part = (self.kept[0], self.arrived[0], self.far[:at], self.far[at], self.far[at - 1])
            self.sent, self.kept = hop([part], self.bits, self.chips, before, True)
            self.move([self.far[at - 1]])

    def last(self):
        return self.kept[0][0] + self.arrived[0][0].astype(jnp.float32)


def groups_of(chips):
    near = [list(range(at, at + 4)) for at in range(0, chips, 4)]
    far = [list(range(at, chips, 4)) for at in range(4)]
    return near, far


def core_half(value, axis, own):
    core = lax.axis_index("ctx")
    size = value.shape[axis] // 2
    which = core if own else 1 - core
    return lax.dynamic_slice_in_dim(value, which * size, size, axis)


def fast_body(
    tokens, lengths, cotangent, projection, mixing, widening, narrowing, biases, widen_bias, norms
):
    chips = lax.axis_size("fsdp")
    core = lax.axis_index("ctx")
    core_at = core.reshape(1)
    bits = dims_of(chips)
    far = bits[:-2]
    down_x = [1, 2] + far[::-1]
    down_y = [2, 1] + far[::-1]
    inputs = tokens[0]
    row_count, model_width = inputs.shape
    shard = projection.shape[0]
    half = model_width // 2
    swap = lambda value: core_permute(value, chips)

    hidden = widen_bias.shape[0] // shard
    rest, packed = pack(core_at, narrowing, mixing, widening, projection, biases, norms, widen_bias.reshape(hidden, shard))
    rest = lax.all_gather(rest, AXES, axis=0, tiled=True).reshape(chips, -1, model_width)
    packed = packed.reshape([1] * len(bits) + [shard, packed.shape[1]])
    cut = packed.shape[-1] // 2
    for mask in far:
        packed = gather_step(packed, chips, mask)
    left = gather_step(packed[..., :cut], chips, 1)
    right = gather_step(packed[..., cut:], chips, 2)
    left_other = chip_permute(left, chips, 2)
    right_other = chip_permute(right, chips, 1)

    narrow_rows = narrowing.shape[0]

    all_inputs = by_core(inputs, swap(inputs), 0)
    inputs_turned = all_inputs.T
    chip_bits = bits_of(chips)
    small_at = 3 * half - cut
    joined, w_own, rows_float = qkv(
        jnp.concatenate([core_at, chip_bits]), all_inputs, left, left_other, right, right_other, small_at
    )
    widen_float = rows_float[8 : 8 + hidden].reshape(hidden, chips, shard).transpose(1, 0, 2).reshape(1, -1)
    mixed_own, logsum = attn_fwd(lengths, joined, [inputs_turned])
    mixed_other = swap(mixed_own)
    first_low, first_turned, normed_one, inverse_one, active_low, slope = widen(
        core_at, mixed_own, mixed_other, rest, narrow_rows, inputs, rows_float, widen_float
    )
    first_other = swap(first_turned)
    active_other = swap(active_low)
    result, grad_two, second_grad, dm_own, dm_other, second_sums = narrow(
        core_at, active_low, rest, narrow_rows, normed_one, rows_float, cotangent[0]
    )

    near, line = groups_of(chips)
    narrow_term = narrow_grad(active_low, active_other, dm_own, swap(dm_other), chips)
    narrow_near = lax.psum_scatter(
        narrow_term, "fsdp", scatter_dimension=0, axis_index_groups=near, tiled=True
    ).reshape(chips // 4, narrow_rows, half)

    (
        expand_own, expand_other, widen_columns, grad_one, branch_grad, branch_other, mixed_grad, mixed_other_grad,
        first_sums,
    ) = back(
        core_at, second_grad, grad_two, normed_one, inverse_one, rows_float,
        rest, narrow_rows, slope, chips, [narrow_term],
    )
    mixed_grad_other = swap(mixed_other_grad)
    branch_other = swap(branch_other)
    widen_terms_two = widen_grad(first_turned, first_other, expand_own, swap(expand_other))
    widen_chain = Chain([term.reshape(chips, shard, -1) for term in widen_terms_two], chips, chip_bits)
    widen_chain.first()

    mixing_term = mixing_grad(core_at, mixed_own, mixed_other, branch_grad, branch_other)

    grad, grad_sums = attn_bwd(
        core_at, lengths, joined, mixed_grad, mixed_grad_other, logsum, widen_chain.sent + [mixing_term]
    )
    narrow_share = lax.psum_scatter(
        narrow_near, "fsdp", scatter_dimension=0, axis_index_groups=line, tiled=True
    )[0].astype(jnp.float32)
    last_terms = last_grad(
        core_at, inputs_turned, grad, mixing_term, grad_sums, first_sums, second_sums, widen_columns
    )
    last_chain = Chain([term.reshape(chips, shard, -1) for term in last_terms], chips, chip_bits)
    last_chain.first()
    widen_chain.second([grad, narrow_near] + last_chain.sent)
    own_part, other_part = tokens_grad(core_at, grad, w_own, grad_one, last_chain.sent + [narrow_share])
    last_chain.second(widen_chain.sent)
    widen_chain.third(last_chain.sent)
    last_chain.third(widen_chain.sent)
    input_grad = own_part + swap(other_part)
    widen_chain.fourth(last_chain.sent)
    last_chain.fourth(widen_chain.sent)
    join = lambda share: by_core(share, swap(share), 1)
    widen_share = join(widen_chain.last())
    narrow_share = join(narrow_share)
    last_share = last_chain.last()
    other_share = swap(last_share)

    grad_projection, grad_mixing, small_share = finish(
        core_at, last_share, other_share, half, [widen_share, narrow_share]
    )
    return (
        result.astype(jnp.bfloat16)[None],
        input_grad[None],
        grad_projection,
        grad_mixing,
        widen_share,
        narrow_share,
        small_share[:4],
        small_share[8 : 8 + hidden].reshape(-1),
        small_share[4:8],
    )


def solution(mesh):
    in_specs = (
        P("fsdp", "ctx", None),
        P("fsdp"),
        P("fsdp", "ctx", None),
        P("fsdp", None),
        P("fsdp", None),
        P("fsdp", None),
        P("fsdp", None),
        P(None, "fsdp"),
        P("fsdp"),
        P(None, "fsdp"),
    )
    out_specs = (
        P("fsdp", "ctx", None),
        P("fsdp", "ctx", None),
        P("fsdp", None),
        P("fsdp", None),
        P("fsdp", None),
        P("fsdp", None),
        P(None, "fsdp"),
        P("fsdp"),
        P(None, "fsdp"),
    )
    chips = mesh.shape["fsdp"]
    paired = mesh.shape["ctx"] == 2 and chips >= 4 and chips & (chips - 1) == 0
    body = fast_body if paired else general_body
    return jax.shard_map(body, mesh=mesh, in_specs=in_specs, out_specs=out_specs, check_vma=False)
```

profile of v0, /device:TPU:0, one launch (start us, length us, event | category | flops | bytes accessed | tf_op | source)
XLA Modules:
  0.0 285.4 jit_solution(1652384189097111811)
XLA Ops:
  7.2 1.3 reshape.89.hidden_ref
  8.5 2.0 pack.1
  10.6 4.1 %collective-permute-start.1 = (bf16[1,1,1,1,48,1280]{5,4,3,2,1,0:T(8,128)(2,1)}, bf16[1,1,1,1,48,1280]{5,4,3,2,1,0:T(8,128)(2,1)S(1)}, u32[]{:S(2)}, u32[]{:S(2)}) collective-permute-start(bf16[1,1,1,1,48,1280]{5,4,3,2,1,0:T(8,128)(2,1)} %bitcast.86), channel_id=1, source_target_pairs={{0,16},{1,17},{2,18},{3,19},{4,20},{5,21},{6,22},{7,23},{8,24},{9,... | collective-permute-start | bytes 368648 | tf_op jit(solution)/shard_map/ppermute | solution.py:944
  14.7 6.2 %collective-permute-done.1 = bf16[1,1,1,1,48,1280]{5,4,3,2,1,0:T(8,128)(2,1)S(1)} collective-permute-done((bf16[1,1,1,1,48,1280]{5,4,3,2,1,0:T(8,128)(2,1)}, bf16[1,1,1,1,48,1280]{5,4,3,2,1,0:T(8,128)(2,1)S(1)}, u32[]{:S(2)}, u32[]{:S(2)}) %collective-permute-start.1) | collective-permute-done | bytes 122912 | tf_op jit(solution)/shard_map/ppermute | solution.py:944
  22.7 10.7 %collective-permute-done.2 = bf16[2,1,1,1,48,1280]{5,4,3,2,1,0:T(8,128)(2,1)S(1)} collective-permute-done((bf16[2,1,1,1,48,1280]{5,4,3,2,1,0:T(8,128)(2,1)S(1)}, bf16[2,1,1,1,48,1280]{5,4,3,2,1,0:T(8,128)(2,1)S(1)}, u32[]{:S(2)}, u32[]{:S(2)}) %collective-permute-start.2) | collective-permute-done | bytes 245792 | tf_op jit(solution)/shard_map/ppermute | solution.py:944
  33.5 1.6 collective-permute-start.3
  36.7 1.5 collective-permute-start.5
  38.2 1.5 collective-permute-done.3
  40.7 1.5 collective-permute-start.4
  42.2 3.3 %collective-permute-done.5 = bf16[2,2,1,1,48,640]{5,4,3,2,1,0:T(8,128)(2,1)S(1)} collective-permute-done((bf16[2,2,1,1,48,640]{5,4,3,2,1,0:T(8,128)(2,1)S(1)}, bf16[2,2,1,1,48,640]{5,4,3,2,1,0:T(8,128)(2,1)S(1)}, u32[]{:S(2)}, u32[]{:S(2)}) %collective-permute-start.5) | collective-permute-done | bytes 245792 | tf_op jit(solution)/shard_map/ppermute | solution.py:944
  47.4 1.6 copy.28.x_ref
  49.0 11.6 %collective-permute-done.4 = bf16[2,2,1,2,48,640]{5,4,3,2,1,0:T(8,128)(2,1)} collective-permute-done((bf16[2,2,1,2,48,640]{5,4,3,2,1,0:T(8,128)(2,1)}, bf16[2,2,1,2,48,640]{5,4,3,2,1,0:T(8,128)(2,1)}, u32[]{:S(2)}, u32[]{:S(2)}) %collective-permute-start.4) | collective-permute-done | bytes 491552 | tf_op jit(solution)/shard_map/ppermute | solution.py:944
  60.6 6.6 %collective-permute-done.6 = bf16[2,2,2,1,48,640]{5,4,3,2,1,0:T(8,128)(2,1)} collective-permute-done((bf16[2,2,2,1,48,640]{5,4,3,2,1,0:T(8,128)(2,1)}, bf16[2,2,2,1,48,640]{5,4,3,2,1,0:T(8,128)(2,1)}, u32[]{:S(2)}, u32[]{:S(2)}) %collective-permute-start.6) | collective-permute-done | bytes 491552 | tf_op jit(solution)/shard_map/ppermute | solution.py:944
  67.3 5.7 %qkv.1 = (bf16[1024,1152]{1,0:T(8,128)(2,1)}, bf16[768,1152]{1,0:T(8,128)(2,1)}, f32[16,768]{1,0:T(8,128)}) custom-call(s32[5]{0:T(128)} %concatenate.25.place_ref, bf16[1024,768]{1,0:T(8,128)(2,1)} %copy.28.x_ref, bf16[4,2,48,640]{3,2,1,0:T(8,128)(2,1)} %bitcast.7.left_ref, bf16[4,2,48,640]{3,2,1,0:T(8,128)(2,1)} %bitcast.8.left_other_ref, ...), custom_call_target="tpu_custom_call" | custom-call | flops 200000000 | bytes 4096 | tf_op jit(solution)/shard_map/qkv/pallas_call | solution.py:863
  73.0 1.7 copy-done.2
  74.6 14.4 %attn_fwd.1 = (bf16[1024,384]{1,0:T(8,128)(2,1)S(1)}, f32[3,2,1024]{2,1,0:T(2,128)S(1)}) custom-call(s32[1]{0:T(128)S(6)} %copy.42.len_ref, bf16[1024,1152]{1,0:T(8,128)(2,1)S(1)} %copy-done.2, bf16[1024,1152]{1,0:T(8,128)(2,1)S(1)} %copy-done.2, bf16[1024,1152]{1,0:T(8,128)(2,1)S(1)} %copy-done.2, bf16[768,1024]{1,0:T(8,128)(2,1)S(1)} %get-tuple-element.117.refs_0_.turned_ref), custom_call_target="tpu_custom_call" | custom-call | flops 725000000 | bytes 4096 | tf_op jit(solution)/shard_map/attn_fwd/pallas_call | solution.py:235
  92.8 19.8 %all-gather.2.cloned.1.call-done = bf16[7168,768]{1,0:T(8,128)(2,1)} async-done(((bf16[224,768]{1,0:T(8,128)(2,1)}), bf16[7168,768]{1,0:T(8,128)(2,1)}) %all-gather.2.cloned.1.call-update) | async-done | bytes 11010064 | tf_op jit(solution)/shard_map/all_gather | solution.py:1127
  112.6 4.1 %copy-done = bf16[7168,768]{1,0:T(8,128)(2,1)S(1)} copy-done((bf16[7168,768]{1,0:T(8,128)(2,1)S(1)}, bf16[7168,768]{1,0:T(8,128)(2,1)}, u32[]{:S(2)}) %copy-start) | copy-done | bytes 11010072
  120.2 10.0 %widen.1 = (bf16[512,768]{1,0:T(8,128)(2,1)}, bf16[768,512]{1,0:T(8,128)(2,1)}, f32[512,768]{1,0:T(8,128)S(1)}, f32[512,1]{1,0:T(8,128)S(1)}, bf16[512,3072]{1,0:T(8,128)(2,1)S(1)}, /*index=5*/f32[512,3072]{1,0:T(8,128)S(1)}) custom-call(s32[1]{0:T(128)} %bitcast.core_ref, bf16[1024,384]{1,0:T(8,128)(2,1)S(1)} %copy-done.17, ...), custom_call_target="tpu_custom_call" | custom-call | flops 625000000 | bytes 4096 | tf_op jit(solution)/shard_map/widen/pallas_call | solution.py:391
  130.2 2.6 copy-done.13
  133.0 6.3 %narrow.1 = (bf16[512,768]{1,0:T(8,128)(2,1)}, f32[512,768]{1,0:T(8,128)S(1)}, bf16[512,768]{1,0:T(8,128)(2,1)S(1)}, bf16[512,384]{1,0:T(8,128)(2,1)S(1)}, bf16[...) custom-call(s32[1]{0:T(128)} %bitcast.core_ref, bf16[512,3072]{1,0:T(8,128)(2,1)S(1)} %get-tuple-element.68.g_ref.own_ref, ...), custom_call_target="tpu_custom_call" | custom-call | flops 400000000 | bytes 4096 | tf_op jit(solution)/shard_map/narrow/pallas_call | solution.py:742
  142.2 1.5 collective-permute-done.9.dm_other_ref
  143.7 5.3 %narrow_grad.1.refs_0_ = bf16[4,4,192,384]{3,2,1,0:T(8,128)(2,1)} custom-call(bf16[512,3072]{1,0:T(8,128)(2,1)S(1)} %get-tuple-element.68.g_ref.own_ref, bf16[512,3072]{1,0:T(8,128)(2,1)S(1)} %collective-permute-done.8.other_ref, bf16[512,384]{1,0:T(8,128)(2,1)S(1)} %get-tuple-element.75.dm_own_ref, bf16[512,384]{1,0:T(8,128)(2,1)S(1)} %collective-permute-done.9.dm_other_ref), custom_call_target="tpu_custom_call" | custom-call | flops 225000000 | bytes 4096 | tf_op jit(solution)/shard_map/narrow_grad/pallas_call | solution.py:789
  149.1 17.5 %back.1 = (bf16[512,1536]{1,0:T(8,128)(2,1)}, bf16[512,1536]{1,0:T(8,128)(2,1)}, f32[768,128]{1,0:T(8,128)}, f32[512,768]{1,0:T(8,128)}, bf16[512,768]{1,0:T(8,1...) custom-call(s32[1]{0:T(128)} %bitcast.core_ref, ...), custom_call_target="tpu_custom_call" | custom-call | flops 690000000 | bytes 4096 | tf_op jit(solution)/shard_map/back/pallas_call | solution.py:501
  167.7 3.7 %collective-permute-done.13.grad_other_ref = bf16[512,384]{1,0:T(8,128)(2,1)S(1)} collective-permute-done((bf16[512,384]{1,0:T(8,128)(2,1)}, bf16[512,384]{1,0:T(8,128)(2,1)S(1)}, u32[]{:S(2)}, u32[]{:S(2)}) %collective-permute-start.13) | collective-permute-done | bytes 393248 | tf_op jit(solution)/shard_map/ppermute | solution.py:939
  175.1 4.8 %widen_grad.1 = (bf16[768,768]{1,0:T(8,128)(2,1)S(1)}, bf16[768,768]{1,0:T(8,128)(2,1)S(1)}) custom-call(bf16[768,512]{1,0:T(8,128)(2,1)} %get-tuple-element.80.own_ref, bf16[768,512]{1,0:T(8,128)(2,1)} %collective-permute-done.11.other_ref, bf16[512,1536]{1,0:T(8,128)(2,1)S(1)} %copy-done.36, bf16[512,1536]{1,0:T(8,128)(2,1)} %collective-permute-done.12.grad_other_ref), custom_call_target="tpu_custom_call" | custom-call | flops 200000000 | bytes 4096 | tf_op jit(solution)/shard_map/widen_grad/pallas_call | solution.py:609
  180.0 1.7 collective-permute-start.17
  182.3 23.9 %attn_bwd.1 = (bf16[1024,1152]{1,0:T(8,128)(2,1)S(1)}, f32[8,1152]{1,0:T(8,128)S(1)}) custom-call(s32[1]{0:T(128)} %bitcast.core_ref, s32[1]{0:T(128)S(6)} %copy.42.len_ref, bf16[1024,1152]{1,0:T(8,128)(2,1)S(1)} %copy-done.3, bf16[1024,1152]{1,0:T(8,128)(2,1)S(1)} %copy-done.3, bf16[1024,1152]{1,0:T(8,128)(2,1)S(1)} %copy-done.3, ...), custom_call_target="tpu_custom_call" | custom-call | flops 1100000000 | bytes 4096 | tf_op jit(solution)/shard_map/attn_bwd/pallas_call | solution.py:307
  206.2 2.7 last_grad.1
  210.9 1.6 collective-permute-start.16
  215.5 1.3 copy-done.9
  220.0 2.0 hop.6
  223.6 1.7 collective-permute-start.21
  225.8 4.2 %collective-permute-done.15.refs_1_.refs_3_ = bf16[8,48,768]{2,1,0:T(8,128)(2,1)} collective-permute-done((bf16[8,48,768]{2,1,0:T(8,128)(2,1)}, bf16[8,48,768]{2,1,0:T(8,128)(2,1)}, u32[]{:S(2)}, u32[]{:S(2)}) %collective-permute-start.15) | collective-permute-done | bytes 589856 | tf_op jit(solution)/shard_map/ppermute | solution.py:944
  230.0 1.4 copy-done.7
  232.6 3.0 %hop.7 = (bf16[4,48,768]{2,1,0:T(8,128)(2,1)S(1)}, f32[4,48,768]{2,1,0:T(8,128)S(1)}, bf16[4,48,896]{2,1,0:T(8,128)(2,1)S(1)}, f32[4,48,896]{2,1,0:T(8,128)S(1)}) custom-call(s32[4]{0:T(128)S(1)} %pad_add_fusion.bits_ref, bf16[16,48,768]{2,1,0:T(8,128)(2,1)S(1)} %bitcast.76, bf16[8,48,768]{2,1,0:T(8,128)(2,1)} %collective-permute-done.15.refs_1_.refs_3_, ...), custom_call_target="tpu_custom_call" | custom-call | flops 100000000 | bytes 4096 | tf_op jit(solution)/shard_map/hop/pallas_call | solution.py:1037
  235.6 1.4 collective-permute-start.20
  238.4 1.4 collective-permute-start.24
  239.8 3.9 %collective-permute-done.19.refs_1_.refs_3_ = bf16[4,48,768]{2,1,0:T(8,128)(2,1)S(1)} collective-permute-done((bf16[4,48,768]{2,1,0:T(8,128)(2,1)S(1)}, bf16[4,48,768]{2,1,0:T(8,128)(2,1)S(1)}, u32[]{:S(2)}, u32[]{:S(2)}) %collective-permute-start.19) | collective-permute-done | bytes 294944 | tf_op jit(solution)/shard_map/ppermute | solution.py:944
  244.5 1.5 collective-permute-start.23
  246.0 4.3 %collective-permute-done.24.refs_1_.refs_3_ = bf16[2,48,1536]{2,1,0:T(8,128)(2,1)S(1)} collective-permute-done((bf16[2,48,1536]{2,1,0:T(8,128)(2,1)S(1)}, bf16[2,48,1536]{2,1,0:T(8,128)(2,1)S(1)}, u32[]{:S(2)}, u32[]{:S(2)}) %collective-permute-start.24) | collective-permute-done | bytes 294944 | tf_op jit(solution)/shard_map/ppermute | solution.py:944
  250.8 1.9 collective-permute-start.27
  252.7 6.3 %collective-permute-done.23.refs_1_.refs_3_ = bf16[2,48,1664]{2,1,0:T(8,128)(2,1)S(1)} collective-permute-done((bf16[2,48,1664]{2,1,0:T(8,128)(2,1)S(1)}, bf16[2,48,1664]{2,1,0:T(8,128)(2,1)S(1)}, u32[]{:S(2)}, u32[]{:S(2)}) %collective-permute-start.23) | collective-permute-done | bytes 319520 | tf_op jit(solution)/shard_map/ppermute | solution.py:944
  261.5 1.5 copy-done.49
  263.0 1.4 copy-done.50
  264.4 5.1 %tokens_grad.1 = (f32[512,768]{1,0:T(8,128)S(1)}, f32[512,768]{1,0:T(8,128)}) custom-call(s32[1]{0:T(128)} %bitcast.core_ref, bf16[1024,1152]{1,0:T(8,128)(2,1)S(1)} %copy-done.5, bf16[768,1152]{1,0:T(8,128)(2,1)S(1)} %copy-done.49, f32[512,768]{1,0:T(8,128)S(1)} %copy-done.50, bf16[8,48,768]{2,1,0:T(8,128)(2,1)} %dynamic-slice_bitcast_fusion.refs_0_.refs_10_, ...), custom_call_target="tpu_custom_call" | custom-call | flops 5000000000 | bytes 4096 | tf_op jit(solution)/shard_map/tokens_grad/pallas_call | solution.py:573
  271.8 2.1 collective-permute-done.29
  276.2 2.7 add_bitcast_fusion
  (177 shorter events, 42.6 us)
Async XLA Ops:
  7.2 105.5 %all-gather.2.cloned.1.call-start = ((), (), s32[]{:S(2)}) async-start(), calls=%async_computation.2 | async-start | bytes 11354112 | tf_op jit(solution)/shard_map/all_gather | solution.py:1127
  10.6 24.5 %copy-start.14 = (bf16[1,512,768]{2,1,0:T(8,128)(2,1)S(1)}, bf16[1,512,768]{2,1,0:T(8,128)(2,1)}, u32[]{:S(2)}) copy-start(bf16[1,512,768]{2,1,0:T(8,128)(2,1)} %param.10) | copy-start | bytes 2359300
  10.6 204.9 %reduce-scatter.7.cloned.1.call-start = ((), (), s32[]{:S(2)}) async-start(), calls=%async_computation.4 | async-start | bytes 2949120
  10.6 10.3 %collective-permute-start.1 = (bf16[1,1,1,1,48,1280]{5,4,3,2,1,0:T(8,128)(2,1)}, bf16[1,1,1,1,48,1280]{5,4,3,2,1,0:T(8,128)(2,1)S(1)}, u32[]{:S(2)}, u32[]{:S(2)}) collective-permute-start(bf16[1,1,1,1,48,1280]{5,4,3,2,1,0:T(8,128)(2,1)} %bitcast.86), channel_id=1, source_target_pairs={{0,16},{1,17},{2,18},{3,19},{4,20},{5,21},{6,22},{7,23},{8,24},{9,... | collective-permute-start | bytes 368648 | tf_op jit(solution)/shard_map/ppermute | solution.py:944
  21.9 11.5 %collective-permute-start.2 = (bf16[2,1,1,1,48,1280]{5,4,3,2,1,0:T(8,128)(2,1)S(1)}, bf16[2,1,1,1,48,1280]{5,4,3,2,1,0:T(8,128)(2,1)S(1)}, u32[]{:S(2)}, u32[]{:S(2)}) collective-permute-start(bf16[2,1,1,1,48,1280]{5,4,3,2,1,0:T(8,128)(2,1)S(1)} %pad_maximum_fusion.6), channel_id=1, source_target_pairs={{0,8},{1,9},{2,10},{3,11},{4,12},{5,13},{6,14},{7,15},{8,0},{9,1},... | collective-permute-start | bytes 737288 | tf_op jit(solution)/shard_map/ppermute | solution.py:944
  33.5 6.3 %collective-permute-start.3 = (bf16[2,2,1,1,48,640]{5,4,3,2,1,0:T(8,128)(2,1)S(1)}, bf16[2,2,1,1,48,640]{5,4,3,2,1,0:T(8,128)(2,1)S(1)}, u32[]{:S(2)}, u32[]{:S(2)}) collective-permute-start(bf16[2,2,1,1,48,640]{5,4,3,2,1,0:T(8,128)(2,1)S(1)} %get-tuple-element.126), channel_id=1, source_target_pairs={{0,2},{1,3},{2,0},{3,1},{4,6},{5,7},{6,4},{7,5},{8,10},{9,11},{10,... | collective-permute-start | bytes 737288 | tf_op jit(solution)/shard_map/ppermute | solution.py:944
  35.4 11.6 %collective-permute-start = (bf16[512,768]{0,1:T(8,128)(2,1)S(1)}, bf16[512,768]{0,1:T(8,128)(2,1)S(1)}, u32[]{:S(2)}, u32[]{:S(2)}) collective-permute-start(bf16[512,768]{0,1:T(8,128)(2,1)S(1)} %bitcast.84), channel_id=1, source_target_pairs={{0,1},{1,0},{2,3},{3,2},{4,5},{5,4},{6,7},{7,6},{8,9},{9,8},{10,11... | collective-permute-start | bytes 2359304 | tf_op jit(solution)/shard_map/ppermute | solution.py:939
  36.7 8.8 %collective-permute-start.5 = (bf16[2,2,1,1,48,640]{5,4,3,2,1,0:T(8,128)(2,1)S(1)}, bf16[2,2,1,1,48,640]{5,4,3,2,1,0:T(8,128)(2,1)S(1)}, u32[]{:S(2)}, u32[]{:S(2)}) collective-permute-start(bf16[2,2,1,1,48,640]{5,4,3,2,1,0:T(8,128)(2,1)S(1)} %get-tuple-element.125), channel_id=1, source_target_pairs={{0,4},{1,5},{2,6},{3,7},{4,0},{5,1},{6,2},{7,3},{8,12},{9,13},{10,... | collective-permute-start | bytes 737288 | tf_op jit(solution)/shard_map/ppermute | solution.py:944
  40.7 19.9 %collective-permute-start.4 = (bf16[2,2,1,2,48,640]{5,4,3,2,1,0:T(8,128)(2,1)}, bf16[2,2,1,2,48,640]{5,4,3,2,1,0:T(8,128)(2,1)}, u32[]{:S(2)}, u32[]{:S(2)}) collective-permute-start(bf16[2,2,1,2,48,640]{5,4,3,2,1,0:T(8,128)(2,1)} %pad_maximum_fusion.3), channel_id=1, source_target_pairs={{0,4},{1,5},{2,6},{3,7},{4,0},{5,1},{6,2},{7,3},{8,12},{9,13},{10,... | collective-permute-start | bytes 1474568 | tf_op jit(solution)/shard_map/ppermute | solution.py:944
  46.4 20.9 %collective-permute-start.6 = (bf16[2,2,2,1,48,640]{5,4,3,2,1,0:T(8,128)(2,1)}, bf16[2,2,2,1,48,640]{5,4,3,2,1,0:T(8,128)(2,1)}, u32[]{:S(2)}, u32[]{:S(2)}) collective-permute-start(bf16[2,2,2,1,48,640]{5,4,3,2,1,0:T(8,128)(2,1)} %pad_maximum_fusion.4), channel_id=1, source_target_pairs={{0,2},{1,3},{2,0},{3,1},{4,6},{5,7},{6,4},{7,5},{8,10},{9,11},{10,... | collective-permute-start | bytes 1474568 | tf_op jit(solution)/shard_map/ppermute | solution.py:944
  74.6 15.9 %copy-start.41 = (f32[16,768]{1,0:T(8,128)S(1)}, f32[16,768]{1,0:T(8,128)}, u32[]{:S(2)}) copy-start(f32[16,768]{1,0:T(8,128)} %get-tuple-element.67.rows_ref) | copy-start | bytes 147460
  89.6 2.3 collective-permute-start.7
  120.2 12.9 %copy-start.1 = (bf16[7168,768]{1,0:T(8,128)(2,1)S(1)}, bf16[7168,768]{1,0:T(8,128)(2,1)}, u32[]{:S(2)}) copy-start(bf16[7168,768]{1,0:T(8,128)(2,1)} %all-gather.2.cloned.1.call-done) | copy-start | bytes 33030148
  120.2 12.9 %copy-start.37 = (bf16[1,512,768]{2,1,0:T(8,128)(2,1)S(1)}, bf16[1,512,768]{2,1,0:T(8,128)(2,1)}, u32[]{:S(2)}) copy-start(bf16[1,512,768]{2,1,0:T(8,128)(2,1)} %param.12) | copy-start | bytes 2359300
  132.8 6.6 %copy-start.12 = (f32[512,768]{1,0:T(8,128)}, f32[512,768]{1,0:T(8,128)S(1)}, u32[]{:S(2)}) copy-start(f32[512,768]{1,0:T(8,128)S(1)} %get-tuple-element.69.normed_ref) | copy-start | bytes 4718596
  132.8 6.6 %copy-start.43 = (f32[512,1]{1,0:T(8,128)}, f32[512,1]{1,0:T(8,128)S(1)}, u32[]{:S(2)}) copy-start(f32[512,1]{1,0:T(8,128)S(1)} %get-tuple-element.73.inverse_ref) | copy-start | bytes 6148
  132.8 10.9 %collective-permute-start.8 = (bf16[512,3072]{1,0:T(8,128)(2,1)S(1)}, bf16[512,3072]{1,0:T(8,128)(2,1)S(1)}, u32[]{:S(2)}, u32[]{:S(2)}) collective-permute-start(bf16[512,3072]{1,0:T(8,128)(2,1)S(1)} %get-tuple-element.68.g_ref.own_ref), channel_id=1, source_target_pairs={{0,1},{1,0},{2,3},{3,2},{4,5},{5,4},{6,7},{7,6},{8,9},{9,8},{10,11... | collective-permute-start | bytes 9437192 | tf_op jit(solution)/shard_map/ppermute | solution.py:939
  142.0 1.7 collective-permute-start.9
  149.1 111.5 %reduce-scatter.5.cloned.1.call-start = ((), (), s32[]{:S(2)}) async-start(), calls=%async_computation.3 | async-start | bytes 737280 | tf_op jit(solution)/shard_map/reduce_scatter | solution.py:1182
  149.1 22.3 %copy-start.18 = (bf16[1024,384]{1,0:T(8,128)(2,1)S(1)}, bf16[1024,384]{1,0:T(8,128)(2,1)}, u32[]{:S(2)}) copy-start(bf16[1024,384]{1,0:T(8,128)(2,1)} %copy-done.16) | copy-start | bytes 2359300
  166.6 8.1 %collective-permute-start.12 = (bf16[512,1536]{1,0:T(8,128)(2,1)}, bf16[512,1536]{1,0:T(8,128)(2,1)}, u32[]{:S(2)}, u32[]{:S(2)}) collective-permute-start(bf16[512,1536]{1,0:T(8,128)(2,1)} %get-tuple-element.82), channel_id=1, source_target_pairs={{0,1},{1,0},{2,3},{3,2},{4,5},{5,4},{6,7},{7,6},{8,9},{9,8},{10,11... | collective-permute-start | bytes 4718600 | tf_op jit(solution)/shard_map/ppermute | solution.py:939
  166.9 7.8 %collective-permute-start.11 = (bf16[768,512]{1,0:T(8,128)(2,1)}, bf16[768,512]{1,0:T(8,128)(2,1)}, u32[]{:S(2)}, u32[]{:S(2)}) collective-permute-start(bf16[768,512]{1,0:T(8,128)(2,1)} %get-tuple-element.80.own_ref), channel_id=1, source_target_pairs={{0,1},{1,0},{2,3},{3,2},{4,5},{5,4},{6,7},{7,6},{8,9},{9,8},{10,11... | collective-permute-start | bytes 2359304 | tf_op jit(solution)/shard_map/ppermute | solution.py:939
  167.2 4.2 %collective-permute-start.13 = (bf16[512,384]{1,0:T(8,128)(2,1)}, bf16[512,384]{1,0:T(8,128)(2,1)S(1)}, u32[]{:S(2)}, u32[]{:S(2)}) collective-permute-start(bf16[512,384]{1,0:T(8,128)(2,1)} %get-tuple-element.86), channel_id=1, source_target_pairs={{0,1},{1,0},{2,3},{3,2},{4,5},{5,4},{6,7},{7,6},{8,9},{9,8},{10,11... | collective-permute-start | bytes 1179656 | tf_op jit(solution)/shard_map/ppermute | solution.py:939
  167.4 14.8 %collective-permute-start.10 = (bf16[512,384]{1,0:T(8,128)(2,1)}, bf16[512,384]{1,0:T(8,128)(2,1)}, u32[]{:S(2)}, u32[]{:S(2)}) collective-permute-start(bf16[512,384]{1,0:T(8,128)(2,1)} %get-tuple-element.78), channel_id=1, source_target_pairs={{0,1},{1,0},{2,3},{3,2},{4,5},{5,4},{6,7},{7,6},{8,9},{9,8},{10,11... | collective-permute-start | bytes 1179656 | tf_op jit(solution)/shard_map/ppermute | solution.py:939
  175.1 7.2 %copy-start.38 = (bf16[512,768]{1,0:T(8,128)(2,1)S(1)}, bf16[512,768]{1,0:T(8,128)(2,1)}, u32[]{:S(2)}) copy-start(bf16[512,768]{1,0:T(8,128)(2,1)} %get-tuple-element.77.do_ref) | copy-start | bytes 2359300
  175.1 7.2 %copy-start.45 = (f32[3,2,1024]{2,1,0:T(2,128)S(1)}, f32[3,2,1024]{2,1,0:T(2,128)}, u32[]{:S(2)}) copy-start(f32[3,2,1024]{2,1,0:T(2,128)} %copy-done.44) | copy-start | bytes 73732
  180.0 33.9 %collective-permute-start.17 = (bf16[8,48,768]{2,1,0:T(8,128)(2,1)S(1)}, bf16[8,48,768]{2,1,0:T(8,128)(2,1)S(1)}, u32[]{:S(2)}, u32[]{:S(2)}) collective-permute-start(bf16[8,48,768]{2,1,0:T(8,128)(2,1)S(1)} %dynamic-slice_bitcast_fusion.1.refs_0_), channel_id=1, source_target_pairs={{0,2},{1,3},{2,0},{3,1},{4,6},{5,7},{6,4},{7,5},{8,10},{9,11},{10,... | collective-permute-start | bytes 1769480 | tf_op jit(solution)/shard_map/ppermute | solution.py:944
  181.7 32.9 %collective-permute-start.18 = (bf16[8,48,768]{2,1,0:T(8,128)(2,1)S(1)}, bf16[8,48,768]{2,1,0:T(8,128)(2,1)S(1)}, u32[]{:S(2)}, u32[]{:S(2)}) collective-permute-start(bf16[8,48,768]{2,1,0:T(8,128)(2,1)S(1)} %bitcast.81), channel_id=1, source_target_pairs={{0,4},{1,5},{2,6},{3,7},{4,0},{5,1},{6,2},{7,3},{8,12},{9,13},{10,... | collective-permute-start | bytes 1769480 | tf_op jit(solution)/shard_map/ppermute | solution.py:944
  182.3 23.9 %copy-start.42 = (f32[768,128]{1,0:T(8,128)S(1)}, f32[768,128]{1,0:T(8,128)}, u32[]{:S(2)}) copy-start(f32[768,128]{1,0:T(8,128)} %get-tuple-element.93.widen_ref) | copy-start | bytes 1179652
  182.3 23.9 %copy-start.47 = (f32[8,768]{1,0:T(8,128)S(1)}, f32[8,768]{1,0:T(8,128)}, u32[]{:S(2)}) copy-start(f32[8,768]{1,0:T(8,128)} %copy-done.46) | copy-start | bytes 73732
  182.3 23.9 %copy-start.48 = (f32[8,768]{1,0:T(8,128)S(1)}, f32[8,768]{1,0:T(8,128)}, u32[]{:S(2)}) copy-start(f32[8,768]{1,0:T(8,128)} %get-tuple-element.91.first_ref) | copy-start | bytes 73732
  208.9 6.6 %copy-start.5 = (bf16[1024,1152]{1,0:T(8,128)(2,1)S(1)}, bf16[1024,1152]{1,0:T(8,128)(2,1)}, u32[]{:S(2)}) copy-start(bf16[1024,1152]{1,0:T(8,128)(2,1)} %copy-done.4) | copy-start | bytes 7077892
  210.9 19.0 %collective-permute-start.16 = (bf16[8,48,896]{2,1,0:T(8,128)(2,1)}, bf16[8,48,896]{2,1,0:T(8,128)(2,1)}, u32[]{:S(2)}, u32[]{:S(2)}) collective-permute-start(bf16[8,48,896]{2,1,0:T(8,128)(2,1)} %bitcast.24.refs_1_.refs_11_), channel_id=1, source_target_pairs={{0,4},{1,5},{2,6},{3,7},{4,0},{5,1},{6,2},{7,3},{8,12},{9,13},{10,... | collective-permute-start | bytes 2064392 | tf_op jit(solution)/shard_map/ppermute | solution.py:944
  213.4 16.5 %collective-permute-start.15 = (bf16[8,48,768]{2,1,0:T(8,128)(2,1)}, bf16[8,48,768]{2,1,0:T(8,128)(2,1)}, u32[]{:S(2)}, u32[]{:S(2)}) collective-permute-start(bf16[8,48,768]{2,1,0:T(8,128)(2,1)} %dynamic-slice_bitcast_fusion.refs_0_.refs_10_), channel_id=1, source_target_pairs={{0,2},{1,3},{2,0},{3,1},{4,6},{5,7},{6,4},{7,5},{8,10},{9,11},{10,... | collective-permute-start | bytes 1769480 | tf_op jit(solution)/shard_map/ppermute | solution.py:944
  223.6 14.0 %collective-permute-start.21 = (bf16[4,48,768]{2,1,0:T(8,128)(2,1)}, bf16[4,48,768]{2,1,0:T(8,128)(2,1)S(1)}, u32[]{:S(2)}, u32[]{:S(2)}) collective-permute-start(bf16[4,48,768]{2,1,0:T(8,128)(2,1)} %get-tuple-element.98.refs_8_), channel_id=1, source_target_pairs={{0,4},{1,5},{2,6},{3,7},{4,0},{5,1},{6,2},{7,3},{8,12},{9,13},{10,... | collective-permute-start | bytes 884744 | tf_op jit(solution)/shard_map/ppermute | solution.py:944
  225.3 12.3 %collective-permute-start.22 = (bf16[4,48,768]{2,1,0:T(8,128)(2,1)}, bf16[4,48,768]{2,1,0:T(8,128)(2,1)S(1)}, u32[]{:S(2)}, u32[]{:S(2)}) collective-permute-start(bf16[4,48,768]{2,1,0:T(8,128)(2,1)} %get-tuple-element.99.refs_9_), channel_id=1, source_target_pairs={{0,2},{1,3},{2,0},{3,1},{4,6},{5,7},{6,4},{7,5},{8,10},{9,11},{10,... | collective-permute-start | bytes 884744 | tf_op jit(solution)/shard_map/ppermute | solution.py:944
  232.6 5.1 %copy-start.27 = (f32[4,48,768]{2,1,0:T(8,128)S(1)}, f32[4,48,768]{2,1,0:T(8,128)}, u32[]{:S(2)}) copy-start(f32[4,48,768]{2,1,0:T(8,128)} %copy-done.26) | copy-start | bytes 1769476
  232.6 5.1 %copy-start.29 = (f32[4,48,768]{2,1,0:T(8,128)S(1)}, f32[4,48,768]{2,1,0:T(8,128)}, u32[]{:S(2)}) copy-start(f32[4,48,768]{2,1,0:T(8,128)} %copy-done.28) | copy-start | bytes 1769476
  235.6 8.1 %collective-permute-start.20 = (bf16[4,48,896]{2,1,0:T(8,128)(2,1)S(1)}, bf16[4,48,896]{2,1,0:T(8,128)(2,1)S(1)}, u32[]{:S(2)}, u32[]{:S(2)}) collective-permute-start(bf16[4,48,896]{2,1,0:T(8,128)(2,1)S(1)} %get-tuple-element.103.refs_9_), channel_id=1, source_target_pairs={{0,2},{1,3},{2,0},{3,1},{4,6},{5,7},{6,4},{7,5},{8,10},{9,11},{10,... | collective-permute-start | bytes 1032200 | tf_op jit(solution)/shard_map/ppermute | solution.py:944
  237.0 6.7 %collective-permute-start.19 = (bf16[4,48,768]{2,1,0:T(8,128)(2,1)S(1)}, bf16[4,48,768]{2,1,0:T(8,128)(2,1)S(1)}, u32[]{:S(2)}, u32[]{:S(2)}) collective-permute-start(bf16[4,48,768]{2,1,0:T(8,128)(2,1)S(1)} %get-tuple-element.101.refs_8_), channel_id=1, source_target_pairs={{0,4},{1,5},{2,6},{3,7},{4,0},{5,1},{6,2},{7,3},{8,12},{9,13},{10,... | collective-permute-start | bytes 884744 | tf_op jit(solution)/shard_map/ppermute | solution.py:944
  238.4 11.8 %collective-permute-start.24 = (bf16[2,48,1536]{2,1,0:T(8,128)(2,1)S(1)}, bf16[2,48,1536]{2,1,0:T(8,128)(2,1)S(1)}, u32[]{:S(2)}, u32[]{:S(2)}) collective-permute-start(bf16[2,48,1536]{2,1,0:T(8,128)(2,1)S(1)} %get-tuple-element.106.refs_8_), channel_id=1, source_target_pairs={{0,8},{1,9},{2,10},{3,11},{4,12},{5,13},{6,14},{7,15},{8,0},{9,1},... | collective-permute-start | bytes 884744 | tf_op jit(solution)/shard_map/ppermute | solution.py:944
  244.5 14.6 %collective-permute-start.23 = (bf16[2,48,1664]{2,1,0:T(8,128)(2,1)S(1)}, bf16[2,48,1664]{2,1,0:T(8,128)(2,1)S(1)}, u32[]{:S(2)}, u32[]{:S(2)}) collective-permute-start(bf16[2,48,1664]{2,1,0:T(8,128)(2,1)S(1)} %get-tuple-element.108.refs_4_), channel_id=1, source_target_pairs={{0,8},{1,9},{2,10},{3,11},{4,12},{5,13},{6,14},{7,15},{8,0},{9,1},... | collective-permute-start | bytes 958472 | tf_op jit(solution)/shard_map/ppermute | solution.py:944
  250.8 9.6 %collective-permute-start.27 = (bf16[1,48,1536]{2,1,0:T(8,128)(2,1)S(1)}, bf16[1,48,1536]{2,1,0:T(8,128)(2,1)S(1)}, u32[]{:S(2)}, u32[]{:S(2)}) collective-permute-start(bf16[1,48,1536]{2,1,0:T(8,128)(2,1)S(1)} %get-tuple-element.110.refs_4_), channel_id=1, source_target_pairs={{0,16},{1,17},{2,18},{3,19},{4,20},{5,21},{6,22},{7,23},{8,24},{9,... | collective-permute-start | bytes 442376 | tf_op jit(solution)/shard_map/ppermute | solution.py:944
  259.7 10.4 %collective-permute-start.25 = (bf16[1,48,1664]{2,1,0:T(8,128)(2,1)S(1)}, bf16[1,48,1664]{2,1,0:T(8,128)(2,1)}, u32[]{:S(2)}, u32[]{:S(2)}) collective-permute-start(bf16[1,48,1664]{2,1,0:T(8,128)(2,1)S(1)} %get-tuple-element.112), channel_id=1, source_target_pairs={{0,16},{1,17},{2,18},{3,19},{4,20},{5,21},{6,22},{7,23},{8,24},{9,... | collective-permute-start | bytes 479240 | tf_op jit(solution)/shard_map/ppermute | solution.py:944
  260.5 10.9 %collective-permute-start.28 = (f32[48,1536]{1,0:T(8,128)S(1)}, f32[48,1536]{1,0:T(8,128)S(1)}, u32[]{:S(2)}, u32[]{:S(2)}) collective-permute-start(f32[48,1536]{1,0:T(8,128)S(1)} %add_bitcast_fusion.2), channel_id=1, source_target_pairs={{0,1},{1,0},{2,3},{3,2},{4,5},{5,4},{6,7},{7,6},{8,9},{9,8},{10,11... | collective-permute-start | bytes 884744 | tf_op jit(solution)/shard_map/ppermute | solution.py:939
  269.6 6.6 %collective-permute-start.14 = (f32[512,768]{1,0:T(8,128)}, f32[512,768]{1,0:T(8,128)}, u32[]{:S(2)}, u32[]{:S(2)}) collective-permute-start(f32[512,768]{1,0:T(8,128)} %get-tuple-element.97), channel_id=1, source_target_pairs={{0,1},{1,0},{2,3},{3,2},{4,5},{5,4},{6,7},{7,6},{8,9},{9,8},{10,11... | collective-permute-start | bytes 4718600 | tf_op jit(solution)/shard_map/ppermute | solution.py:939
  271.1 3.0 %collective-permute-start.26 = (f32[48,1664]{1,0:T(8,128)S(1)}, f32[48,1664]{1,0:T(8,128)S(1)}, u32[]{:S(2)}, u32[]{:S(2)}) collective-permute-start(f32[48,1664]{1,0:T(8,128)S(1)} %add_bitcast_fusion.1.own_ref), channel_id=1, source_target_pairs={{0,1},{1,0},{2,3},{3,2},{4,5},{5,4},{6,7},{7,6},{8,9},{9,8},{10,11... | collective-permute-start | bytes 958472 | tf_op jit(solution)/shard_map/ppermute | solution.py:939
  271.4 2.6 collective-permute-start.29
  (37 other events, 62.2 us)
Sparse Core Ops, SparseCore 0:
  11.5 101.1 all-gather.1
  149.2 36.6 reduce-scatter.6
  225.9 22.7 reduce-scatter.4
where the time goes:
time: 286 us; the launch traced here: 285 us
  Pallas kernels  107 us (37%)
  waiting for transfers between devices  87 us (30%)
  local copies, waits for them, and re-layouts  41 us (14%)
  starting transfers between devices  26.9 us (9%)
  between operations  14.9 us (5%)
  other arithmetic  8.3 us (3%)
    ppermute x18, waiting for transfers between devices, chip_permute(): return lax.ppermute(value, AXES, pairs)  58.7 us
    unnamed x105, local copies, waits for them, and re-layouts  34.2 us
    ppermute x18, starting transfers between devices, chip_permute(): return lax.ppermute(value, AXES, pairs)  24 us
    pallas_call x1, Pallas kernels, attn_bwd(): pl.pallas_call(attn_bwd_kernel, grid_spec=pltpu.PrefetchScalarGridSpec(nu...  23.9 us
    all_gather x1, waiting for transfers between devices, fast_body(): lax.all_gather(rest, AXES, axis=0, tiled=True)  19.8 us
    pallas_call x1, Pallas kernels, back(): pl.pallas_call(functools.partial(back_kernel, spare=len(before)), grid_sp...  17.5 us
    pallas_call x1, Pallas kernels, attn_fwd(): pl.pallas_call(attn_fwd_kernel, grid=(pairs, L // QB), in_specs=[pl.Block...  14.4 us
    pallas_call x1, Pallas kernels, widen(): pl.pallas_call(widen_kernel, grid_spec=pltpu.PrefetchScalarGridSpec(num_s...  10 us
  transfers between devices with their start and end apart: 33, of which 15 were waited for; matrix products, arithmetic and copies ran while one was open for 4% of the time, Pallas kernels for 31%

commit v1 on v0

--- a/solution.py
+++ b/solution.py
@@ -870,7 +870,7 @@
             jax.ShapeDtypeStruct((16, width), jnp.float32),
         ],
         scratch_shapes=[pltpu.VMEM((width, 128), jnp.float32)],
-        compiler_params=pltpu.CompilerParams(vmem_limit_bytes=56 * 2**20),
+        compiler_params=pltpu.CompilerParams(vmem_limit_bytes=16 * 2**20),
         cost_estimate=cost(4.0),
         name="qkv",
     )(place, inputs, left, left_other, right, right_other)

time: 286 us -> 283 us (0.990)
  waiting for transfers between devices: 87 us -> 82.6 us
    ppermute x18, waiting for transfers between devices: 58.7 us -> 54.8 us  [chip_permute(): return lax.ppermute(value, AXES, pairs)]
    unnamed x105 -> x119, local copies, waits for them, and re-layouts: 34.2 us -> 33.9 us
  transfers between devices with their start and end apart: 33 -> 33, of which waited for: 15 -> 16; matrix products, arithmetic and copies ran while one was open for 4% -> 5% of each run, Pallas kernels for 31% -> 32%
where the time goes in v1:
time: 283 us; the launch traced here: 282 us
  Pallas kernels  107 us (38%)
  waiting for transfers between devices  82.6 us (29%)
  local copies, waits for them, and re-layouts  41.2 us (15%)
  starting transfers between devices  26.8 us (9%)
  between operations  15 us (5%)
  other arithmetic  9.79 us (3%)
    ppermute x18, waiting for transfers between devices, chip_permute(): return lax.ppermute(value, AXES, pairs)  54.8 us
    unnamed x119, local copies, waits for them, and re-layouts  33.9 us
    pallas_call x1, Pallas kernels, attn_bwd(): pl.pallas_call(attn_bwd_kernel, grid_spec=pltpu.PrefetchScalarGridSpec(nu...  24 us
    ppermute x18, starting transfers between devices, chip_permute(): return lax.ppermute(value, AXES, pairs)  23.9 us
    all_gather x1, waiting for transfers between devices, fast_body(): lax.all_gather(rest, AXES, axis=0, tiled=True)  17.5 us
    pallas_call x1, Pallas kernels, back(): pl.pallas_call(functools.partial(back_kernel, spare=len(before)), grid_sp...  17.4 us
    pallas_call x1, Pallas kernels, attn_fwd(): pl.pallas_call(attn_fwd_kernel, grid=(pairs, L // QB), in_specs=[pl.Block...  15 us
    pallas_call x1, Pallas kernels, widen(): pl.pallas_call(widen_kernel, grid_spec=pltpu.PrefetchScalarGridSpec(num_s...  10.8 us
  transfers between devices with their start and end apart: 33, of which 16 were waited for; matrix products, arithmetic and copies ran while one was open for 5% of the time, Pallas kernels for 32%

profile of v1, /device:TPU:0, one launch (start us, length us, event | category | flops | bytes accessed | tf_op | source)
XLA Modules:
  0.0 282.1 jit_solution(12074888799746671044)
XLA Ops:
  7.2 1.3 reshape.89.hidden_ref
  8.5 2.0 pack.1
  10.6 4.1 %collective-permute-start.1 = (bf16[1,1,1,1,48,1280]{5,4,3,2,1,0:T(8,128)(2,1)}, bf16[1,1,1,1,48,1280]{5,4,3,2,1,0:T(8,128)(2,1)S(1)}, u32[]{:S(2)}, u32[]{:S(2)}) collective-permute-start(bf16[1,1,1,1,48,1280]{5,4,3,2,1,0:T(8,128)(2,1)} %bitcast.89), channel_id=1, source_target_pairs={{0,16},{1,17},{2,18},{3,19},{4,20},{5,21},{6,22},{7,23},{8,24},{9,... | collective-permute-start | bytes 368648 | tf_op jit(solution)/shard_map/ppermute | solution.py:944
  14.7 6.2 %collective-permute-done.1 = bf16[1,1,1,1,48,1280]{5,4,3,2,1,0:T(8,128)(2,1)S(1)} collective-permute-done((bf16[1,1,1,1,48,1280]{5,4,3,2,1,0:T(8,128)(2,1)}, bf16[1,1,1,1,48,1280]{5,4,3,2,1,0:T(8,128)(2,1)S(1)}, u32[]{:S(2)}, u32[]{:S(2)}) %collective-permute-start.1) | collective-permute-done | bytes 122912 | tf_op jit(solution)/shard_map/ppermute | solution.py:944
  22.7 10.7 %collective-permute-done.2 = bf16[2,1,1,1,48,1280]{5,4,3,2,1,0:T(8,128)(2,1)S(1)} collective-permute-done((bf16[2,1,1,1,48,1280]{5,4,3,2,1,0:T(8,128)(2,1)S(1)}, bf16[2,1,1,1,48,1280]{5,4,3,2,1,0:T(8,128)(2,1)S(1)}, u32[]{:S(2)}, u32[]{:S(2)}) %collective-permute-start.2) | collective-permute-done | bytes 245792 | tf_op jit(solution)/shard_map/ppermute | solution.py:944
  33.5 1.6 collective-permute-start.3
  37.0 1.5 collective-permute-start.5
  39.9 1.6 collective-permute-start.4
  41.5 4.2 %collective-permute-done.5 = bf16[2,2,1,1,48,640]{5,4,3,2,1,0:T(8,128)(2,1)S(1)} collective-permute-done((bf16[2,2,1,1,48,640]{5,4,3,2,1,0:T(8,128)(2,1)S(1)}, bf16[2,2,1,1,48,640]{5,4,3,2,1,0:T(8,128)(2,1)S(1)}, u32[]{:S(2)}, u32[]{:S(2)}) %collective-permute-start.5) | collective-permute-done | bytes 245792 | tf_op jit(solution)/shard_map/ppermute | solution.py:944
  46.5 1.5 broadcast_select_fusion.1
  48.0 2.1 fusion.1
  50.1 2.6 copy.28.x_ref
  52.7 8.1 %collective-permute-done.4 = bf16[2,2,1,2,48,640]{5,4,3,2,1,0:T(8,128)(2,1)S(1)} collective-permute-done((bf16[2,2,1,2,48,640]{5,4,3,2,1,0:T(8,128)(2,1)S(1)}, bf16[2,2,1,2,48,640]{5,4,3,2,1,0:T(8,128)(2,1)S(1)}, u32[]{:S(2)}, u32[]{:S(2)}) %collective-permute-start.4) | collective-permute-done | bytes 491552 | tf_op jit(solution)/shard_map/ppermute | solution.py:944
  61.6 5.6 %collective-permute-done.6 = bf16[2,2,2,1,48,640]{5,4,3,2,1,0:T(8,128)(2,1)S(1)} collective-permute-done((bf16[2,2,2,1,48,640]{5,4,3,2,1,0:T(8,128)(2,1)S(1)}, bf16[2,2,2,1,48,640]{5,4,3,2,1,0:T(8,128)(2,1)S(1)}, u32[]{:S(2)}, u32[]{:S(2)}) %collective-permute-start.6) | collective-permute-done | bytes 491552 | tf_op jit(solution)/shard_map/ppermute | solution.py:944
  67.9 1.4 copy-done.15
  73.5 2.9 %qkv.1 = (bf16[1024,1152]{1,0:T(8,128)(2,1)S(1)}, bf16[768,1152]{1,0:T(8,128)(2,1)S(1)}, f32[16,768]{1,0:T(8,128)S(1)}) custom-call(s32[5]{0:T(128)S(1)} %concatenate.25.place_ref, bf16[1024,768]{1,0:T(8,128)(2,1)S(1)} %copy-done.15, bf16[4,2,48,640]{3,2,1,0:T(8,128)(2,1)S(1)} %bitcast.83, bf16[4,2,48,640]{3,2,1,0:T(8,128)(2,1)S(1)} %bitcast.86, ...), custom_call_target="tpu_custom_call" | custom-call | flops 200000000 | bytes 4096 | tf_op jit(solution)/shard_map/qkv/pallas_call | solution.py:863
  77.6 15.0 %attn_fwd.1 = (bf16[1024,384]{1,0:T(8,128)(2,1)}, f32[3,2,1024]{2,1,0:T(2,128)S(1)}) custom-call(s32[1]{0:T(128)S(6)} %copy.42.len_ref, bf16[1024,1152]{1,0:T(8,128)(2,1)S(1)} %get-tuple-element.64.q_ref.k_ref.v_ref, bf16[1024,1152]{1,0:T(8,128)(2,1)S(1)} %get-tuple-element.64.q_ref.k_ref.v_ref, bf16[1024,1152]{1,0:T(8,128)(2,1)S(1)} %get-tuple-element.64.q_ref.k_ref.v_ref, ...), custom_call_target="tpu_custom_call" | custom-call | flops 725000000 | bytes 4096 | tf_op jit(solution)/shard_map/attn_fwd/pallas_call | solution.py:235
  93.4 2.4 collective-permute-done.7.other_ref
  95.9 17.5 %all-gather.2.cloned.1.call-done = bf16[7168,768]{1,0:T(8,128)(2,1)} async-done(((bf16[224,768]{1,0:T(8,128)(2,1)}), bf16[7168,768]{1,0:T(8,128)(2,1)}) %all-gather.2.cloned.1.call-update) | async-done | bytes 11010064 | tf_op jit(solution)/shard_map/all_gather | solution.py:1127
  113.3 4.1 %copy-done = bf16[7168,768]{1,0:T(8,128)(2,1)S(1)} copy-done((bf16[7168,768]{1,0:T(8,128)(2,1)S(1)}, bf16[7168,768]{1,0:T(8,128)(2,1)}, u32[]{:S(2)}) %copy-start) | copy-done | bytes 11010072
  117.5 10.8 %widen.1 = (bf16[512,768]{1,0:T(8,128)(2,1)}, bf16[768,512]{1,0:T(8,128)(2,1)S(1)}, f32[512,768]{1,0:T(8,128)S(1)}, f32[512,1]{1,0:T(8,128)S(1)}, bf16[512,3072]...) custom-call(s32[1]{0:T(128)} %bitcast.core_ref, bf16[1024,384]{1,0:T(8,128)(2,1)} %get-tuple-element.65.own_ref, ...), custom_call_target="tpu_custom_call" | custom-call | flops 625000000 | bytes 4096 | tf_op jit(solution)/shard_map/widen/pallas_call | solution.py:391
  128.6 6.3 %narrow.1 = (bf16[512,768]{1,0:T(8,128)(2,1)}, f32[512,768]{1,0:T(8,128)S(1)}, bf16[512,768]{1,0:T(8,128)(2,1)S(1)}, bf16[512,384]{1,0:T(8,128)(2,1)S(1)}, bf16[...) custom-call(s32[1]{0:T(128)} %bitcast.core_ref, bf16[512,3072]{1,0:T(8,128)(2,1)S(1)} %get-tuple-element.68.g_ref.own_ref, ...), custom_call_target="tpu_custom_call" | custom-call | flops 400000000 | bytes 4096 | tf_op jit(solution)/shard_map/narrow/pallas_call | solution.py:742
  137.9 1.5 collective-permute-done.9.dm_other_ref
  139.4 4.7 %narrow_grad.1.refs_0_ = bf16[4,4,192,384]{3,2,1,0:T(8,128)(2,1)S(1)} custom-call(bf16[512,3072]{1,0:T(8,128)(2,1)S(1)} %get-tuple-element.68.g_ref.own_ref, bf16[512,3072]{1,0:T(8,128)(2,1)S(1)} %collective-permute-done.8.other_ref, bf16[512,384]{1,0:T(8,128)(2,1)S(1)} %get-tuple-element.75.dm_own_ref, bf16[512,384]{1,0:T(8,128)(2,1)S(1)} %collective-permute-done.9.dm_other_ref), custom_call_target="tpu_custom_call" | custom-call | flops 225000000 | bytes 4096 | tf_op jit(solution)/shard_map/narrow_grad/pallas_call | solution.py:789
  144.1 1.4 copy-done.2
  145.6 17.4 %back.1 = (bf16[512,1536]{1,0:T(8,128)(2,1)}, bf16[512,1536]{1,0:T(8,128)(2,1)}, f32[768,128]{1,0:T(8,128)}, f32[512,768]{1,0:T(8,128)}, bf16[512,768]{1,0:T(8,1...) custom-call(s32[1]{0:T(128)} %bitcast.core_ref, ...), custom_call_target="tpu_custom_call" | custom-call | flops 690000000 | bytes 4096 | tf_op jit(solution)/shard_map/back/pallas_call | solution.py:501
  164.1 4.3 %collective-permute-done.13.grad_other_ref = bf16[512,384]{1,0:T(8,128)(2,1)S(1)} collective-permute-done((bf16[512,384]{1,0:T(8,128)(2,1)}, bf16[512,384]{1,0:T(8,128)(2,1)S(1)}, u32[]{:S(2)}, u32[]{:S(2)}) %collective-permute-start.13) | collective-permute-done | bytes 393248 | tf_op jit(solution)/shard_map/ppermute | solution.py:939
  169.5 2.5 mixing_grad.1.refs_2_.mixing_ref
  172.1 4.5 %widen_grad.1 = (bf16[768,768]{1,0:T(8,128)(2,1)S(1)}, bf16[768,768]{1,0:T(8,128)(2,1)S(1)}) custom-call(bf16[768,512]{1,0:T(8,128)(2,1)S(1)} %copy-done.39, bf16[768,512]{1,0:T(8,128)(2,1)} %collective-permute-done.11.other_ref, bf16[512,1536]{1,0:T(8,128)(2,1)S(1)} %copy-done.35, bf16[512,1536]{1,0:T(8,128)(2,1)} %collective-permute-done.12.grad_other_ref), custom_call_target="tpu_custom_call" | custom-call | flops 200000000 | bytes 4096 | tf_op jit(solution)/shard_map/widen_grad/pallas_call | solution.py:609
  176.7 1.5 collective-permute-start.17
  179.3 24.0 %attn_bwd.1 = (bf16[1024,1152]{1,0:T(8,128)(2,1)S(1)}, f32[8,1152]{1,0:T(8,128)S(1)}) custom-call(s32[1]{0:T(128)} %bitcast.core_ref, s32[1]{0:T(128)S(6)} %copy.42.len_ref, bf16[1024,1152]{1,0:T(8,128)(2,1)S(1)} %get-tuple-element.64.q_ref.k_ref.v_ref, bf16[1024,1152]{1,0:T(8,128)(2,1)S(1)} %get-tuple-element.64.q_ref.k_ref.v_ref, ...), custom_call_target="tpu_custom_call" | custom-call | flops 1100000000 | bytes 4096 | tf_op jit(solution)/shard_map/attn_bwd/pallas_call | solution.py:307
  203.4 2.7 last_grad.1
  216.9 2.0 hop.6
  220.5 1.5 collective-permute-start.21
  223.0 3.1 %collective-permute-done.15.refs_1_.refs_3_ = bf16[8,48,768]{2,1,0:T(8,128)(2,1)} collective-permute-done((bf16[8,48,768]{2,1,0:T(8,128)(2,1)}, bf16[8,48,768]{2,1,0:T(8,128)(2,1)}, u32[]{:S(2)}, u32[]{:S(2)}) %collective-permute-start.15) | collective-permute-done | bytes 589856 | tf_op jit(solution)/shard_map/ppermute | solution.py:944
  226.8 1.4 copy-done.8
  229.4 3.0 %hop.7 = (bf16[4,48,768]{2,1,0:T(8,128)(2,1)S(1)}, f32[4,48,768]{2,1,0:T(8,128)S(1)}, bf16[4,48,896]{2,1,0:T(8,128)(2,1)S(1)}, f32[4,48,896]{2,1,0:T(8,128)S(1)}) custom-call(s32[4]{0:T(128)S(1)} %pad_add_fusion.bits_ref, bf16[16,48,768]{2,1,0:T(8,128)(2,1)S(1)} %bitcast.76, bf16[8,48,768]{2,1,0:T(8,128)(2,1)} %collective-permute-done.15.refs_1_.refs_3_, ...), custom_call_target="tpu_custom_call" | custom-call | flops 100000000 | bytes 4096 | tf_op jit(solution)/shard_map/hop/pallas_call | solution.py:1037
  234.9 1.3 collective-permute-start.24
  236.2 4.1 %collective-permute-done.19.refs_1_.refs_3_ = bf16[4,48,768]{2,1,0:T(8,128)(2,1)S(1)} collective-permute-done((bf16[4,48,768]{2,1,0:T(8,128)(2,1)S(1)}, bf16[4,48,768]{2,1,0:T(8,128)(2,1)S(1)}, u32[]{:S(2)}, u32[]{:S(2)}) %collective-permute-start.19) | collective-permute-done | bytes 294944 | tf_op jit(solution)/shard_map/ppermute | solution.py:944
  241.1 1.3 collective-permute-start.23
  242.4 4.7 %collective-permute-done.24.refs_1_.refs_3_ = bf16[2,48,1536]{2,1,0:T(8,128)(2,1)S(1)} collective-permute-done((bf16[2,48,1536]{2,1,0:T(8,128)(2,1)S(1)}, bf16[2,48,1536]{2,1,0:T(8,128)(2,1)S(1)}, u32[]{:S(2)}, u32[]{:S(2)}) %collective-permute-start.24) | collective-permute-done | bytes 294944 | tf_op jit(solution)/shard_map/ppermute | solution.py:944
  247.7 2.2 collective-permute-start.27
  249.9 6.0 %collective-permute-done.23.refs_1_.refs_3_ = bf16[2,48,1664]{2,1,0:T(8,128)(2,1)S(1)} collective-permute-done((bf16[2,48,1664]{2,1,0:T(8,128)(2,1)S(1)}, bf16[2,48,1664]{2,1,0:T(8,128)(2,1)S(1)}, u32[]{:S(2)}, u32[]{:S(2)}) %collective-permute-start.23) | collective-permute-done | bytes 319520 | tf_op jit(solution)/shard_map/ppermute | solution.py:944
  258.2 1.5 copy-done.56
  259.7 1.4 copy-done.57
  261.1 5.1 %tokens_grad.1 = (f32[512,768]{1,0:T(8,128)S(1)}, f32[512,768]{1,0:T(8,128)}) custom-call(s32[1]{0:T(128)} %bitcast.core_ref, bf16[1024,1152]{1,0:T(8,128)(2,1)S(1)} %copy-done.6, bf16[768,1152]{1,0:T(8,128)(2,1)S(1)} %copy-done.56, f32[512,768]{1,0:T(8,128)S(1)} %copy-done.57, bf16[8,48,768]{2,1,0:T(8,128)(2,1)} %dynamic-slice_bitcast_fusion.refs_0_.refs_10_, ...), custom_call_target="tpu_custom_call" | custom-call | flops 5000000000 | bytes 4096 | tf_op jit(solution)/shard_map/tokens_grad/pallas_call | solution.py:573
  268.5 2.1 collective-permute-done.29
  272.8 2.7 add_bitcast_fusion
  (191 shorter events, 45.5 us)
Async XLA Ops:
  7.2 106.2 %all-gather.2.cloned.1.call-start = ((), (), s32[]{:S(2)}) async-start(), calls=%async_computation.2 | async-start | bytes 11354112 | tf_op jit(solution)/shard_map/all_gather | solution.py:1127
  10.6 24.5 %copy-start.16 = (bf16[1,512,768]{2,1,0:T(8,128)(2,1)S(1)}, bf16[1,512,768]{2,1,0:T(8,128)(2,1)}, u32[]{:S(2)}) copy-start(bf16[1,512,768]{2,1,0:T(8,128)(2,1)} %param.10) | copy-start | bytes 2359300
  10.6 201.8 %reduce-scatter.7.cloned.1.call-start = ((), (), s32[]{:S(2)}) async-start(), calls=%async_computation.4 | async-start | bytes 2949120
  10.6 10.3 %collective-permute-start.1 = (bf16[1,1,1,1,48,1280]{5,4,3,2,1,0:T(8,128)(2,1)}, bf16[1,1,1,1,48,1280]{5,4,3,2,1,0:T(8,128)(2,1)S(1)}, u32[]{:S(2)}, u32[]{:S(2)}) collective-permute-start(bf16[1,1,1,1,48,1280]{5,4,3,2,1,0:T(8,128)(2,1)} %bitcast.89), channel_id=1, source_target_pairs={{0,16},{1,17},{2,18},{3,19},{4,20},{5,21},{6,22},{7,23},{8,24},{9,... | collective-permute-start | bytes 368648 | tf_op jit(solution)/shard_map/ppermute | solution.py:944
  21.9 11.5 %collective-permute-start.2 = (bf16[2,1,1,1,48,1280]{5,4,3,2,1,0:T(8,128)(2,1)S(1)}, bf16[2,1,1,1,48,1280]{5,4,3,2,1,0:T(8,128)(2,1)S(1)}, u32[]{:S(2)}, u32[]{:S(2)}) collective-permute-start(bf16[2,1,1,1,48,1280]{5,4,3,2,1,0:T(8,128)(2,1)S(1)} %pad_maximum_fusion.6), channel_id=1, source_target_pairs={{0,8},{1,9},{2,10},{3,11},{4,12},{5,13},{6,14},{7,15},{8,0},{9,1},... | collective-permute-start | bytes 737288 | tf_op jit(solution)/shard_map/ppermute | solution.py:944
  33.5 6.3 %collective-permute-start.3 = (bf16[2,2,1,1,48,640]{5,4,3,2,1,0:T(8,128)(2,1)S(1)}, bf16[2,2,1,1,48,640]{5,4,3,2,1,0:T(8,128)(2,1)S(1)}, u32[]{:S(2)}, u32[]{:S(2)}) collective-permute-start(bf16[2,2,1,1,48,640]{5,4,3,2,1,0:T(8,128)(2,1)S(1)} %get-tuple-element.126), channel_id=1, source_target_pairs={{0,2},{1,3},{2,0},{3,1},{4,6},{5,7},{6,4},{7,5},{8,10},{9,11},{10,... | collective-permute-start | bytes 737288 | tf_op jit(solution)/shard_map/ppermute | solution.py:944
  36.2 10.2 %collective-permute-start = (bf16[512,768]{0,1:T(8,128)(2,1)}, bf16[512,768]{0,1:T(8,128)(2,1)}, u32[]{:S(2)}, u32[]{:S(2)}) collective-permute-start(bf16[512,768]{0,1:T(8,128)(2,1)} %bitcast.5), channel_id=1, source_target_pairs={{0,1},{1,0},{2,3},{3,2},{4,5},{5,4},{6,7},{7,6},{8,9},{9,8},{10,11... | collective-permute-start | bytes 2359304 | tf_op jit(solution)/shard_map/ppermute | solution.py:939
  37.0 8.8 %collective-permute-start.5 = (bf16[2,2,1,1,48,640]{5,4,3,2,1,0:T(8,128)(2,1)S(1)}, bf16[2,2,1,1,48,640]{5,4,3,2,1,0:T(8,128)(2,1)S(1)}, u32[]{:S(2)}, u32[]{:S(2)}) collective-permute-start(bf16[2,2,1,1,48,640]{5,4,3,2,1,0:T(8,128)(2,1)S(1)} %get-tuple-element.125), channel_id=1, source_target_pairs={{0,4},{1,5},{2,6},{3,7},{4,0},{5,1},{6,2},{7,3},{8,12},{9,13},{10,... | collective-permute-start | bytes 737288 | tf_op jit(solution)/shard_map/ppermute | solution.py:944
  39.9 8.1 %copy-start.28 = (bf16[2,2,1,2,48,640]{5,4,3,2,1,0:T(8,128)(2,1)}, bf16[2,2,1,2,48,640]{5,4,3,2,1,0:T(8,128)(2,1)S(1)}, u32[]{:S(2)}) copy-start(bf16[2,2,1,2,48,640]{5,4,3,2,1,0:T(8,128)(2,1)S(1)} %pad_maximum_fusion.3) | copy-start | bytes 1474564
  39.9 20.9 %collective-permute-start.4 = (bf16[2,2,1,2,48,640]{5,4,3,2,1,0:T(8,128)(2,1)S(1)}, bf16[2,2,1,2,48,640]{5,4,3,2,1,0:T(8,128)(2,1)S(1)}, u32[]{:S(2)}, u32[]{:S(2)}) collective-permute-start(bf16[2,2,1,2,48,640]{5,4,3,2,1,0:T(8,128)(2,1)S(1)} %pad_maximum_fusion.3), channel_id=1, source_target_pairs={{0,4},{1,5},{2,6},{3,7},{4,0},{5,1},{6,2},{7,3},{8,12},{9,13},{10,... | collective-permute-start | bytes 1474568 | tf_op jit(solution)/shard_map/ppermute | solution.py:944
  45.9 21.3 %collective-permute-start.6 = (bf16[2,2,2,1,48,640]{5,4,3,2,1,0:T(8,128)(2,1)S(1)}, bf16[2,2,2,1,48,640]{5,4,3,2,1,0:T(8,128)(2,1)S(1)}, u32[]{:S(2)}, u32[]{:S(2)}) collective-permute-start(bf16[2,2,2,1,48,640]{5,4,3,2,1,0:T(8,128)(2,1)S(1)} %pad_maximum_fusion.4), channel_id=1, source_target_pairs={{0,2},{1,3},{2,0},{3,1},{4,6},{5,7},{6,4},{7,5},{8,10},{9,11},{10,... | collective-permute-start | bytes 1474568 | tf_op jit(solution)/shard_map/ppermute | solution.py:944
  77.6 51.0 %copy-start.43 = (f32[16,768]{1,0:T(8,128)}, f32[16,768]{1,0:T(8,128)S(1)}, u32[]{:S(2)}) copy-start(f32[16,768]{1,0:T(8,128)S(1)} %get-tuple-element.67.rows_ref) | copy-start | bytes 147460
  93.2 2.6 collective-permute-start.7
  117.5 11.2 %copy-start.1 = (bf16[7168,768]{1,0:T(8,128)(2,1)S(1)}, bf16[7168,768]{1,0:T(8,128)(2,1)}, u32[]{:S(2)}) copy-start(bf16[7168,768]{1,0:T(8,128)(2,1)} %all-gather.2.cloned.1.call-done) | copy-start | bytes 33030148
  117.5 11.2 %copy-start.36 = (bf16[1,512,768]{2,1,0:T(8,128)(2,1)S(1)}, bf16[1,512,768]{2,1,0:T(8,128)(2,1)}, u32[]{:S(2)}) copy-start(bf16[1,512,768]{2,1,0:T(8,128)(2,1)} %param.12) | copy-start | bytes 2359300
  128.3 6.7 %copy-start.13 = (f32[512,768]{1,0:T(8,128)}, f32[512,768]{1,0:T(8,128)S(1)}, u32[]{:S(2)}) copy-start(f32[512,768]{1,0:T(8,128)S(1)} %get-tuple-element.69.normed_ref) | copy-start | bytes 4718596
  128.3 6.7 %copy-start.14 = (f32[512,3072]{1,0:T(8,128)}, f32[512,3072]{1,0:T(8,128)S(1)}, u32[]{:S(2)}) copy-start(f32[512,3072]{1,0:T(8,128)S(1)} %get-tuple-element.74.gp_ref) | copy-start | bytes 18874372
  128.3 6.7 %copy-start.37 = (bf16[768,512]{1,0:T(8,128)(2,1)}, bf16[768,512]{1,0:T(8,128)(2,1)S(1)}, u32[]{:S(2)}) copy-start(bf16[768,512]{1,0:T(8,128)(2,1)S(1)} %get-tuple-element.80.own_ref) | copy-start | bytes 2359300
  128.3 6.7 %copy-start.49 = (f32[512,1]{1,0:T(8,128)}, f32[512,1]{1,0:T(8,128)S(1)}, u32[]{:S(2)}) copy-start(f32[512,1]{1,0:T(8,128)S(1)} %get-tuple-element.73.inverse_ref) | copy-start | bytes 6148
  128.3 11.1 %collective-permute-start.8 = (bf16[512,3072]{1,0:T(8,128)(2,1)S(1)}, bf16[512,3072]{1,0:T(8,128)(2,1)S(1)}, u32[]{:S(2)}, u32[]{:S(2)}) collective-permute-start(bf16[512,3072]{1,0:T(8,128)(2,1)S(1)} %get-tuple-element.68.g_ref.own_ref), channel_id=1, source_target_pairs={{0,1},{1,0},{2,3},{3,2},{4,5},{5,4},{6,7},{7,6},{8,9},{9,8},{10,11... | collective-permute-start | bytes 9437192 | tf_op jit(solution)/shard_map/ppermute | solution.py:939
  137.7 1.7 collective-permute-start.9
  145.5 111.7 %reduce-scatter.5.cloned.1.call-start = ((), (), s32[]{:S(2)}) async-start(), calls=%async_computation.3 | async-start | bytes 737280 | tf_op jit(solution)/shard_map/reduce_scatter | solution.py:1182
  145.6 17.8 %copy-start.38 = (bf16[768,512]{1,0:T(8,128)(2,1)S(1)}, bf16[768,512]{1,0:T(8,128)(2,1)}, u32[]{:S(2)}) copy-start(bf16[768,512]{1,0:T(8,128)(2,1)} %copy-done.37) | copy-start | bytes 2359300
  163.0 9.1 %collective-permute-start.12 = (bf16[512,1536]{1,0:T(8,128)(2,1)}, bf16[512,1536]{1,0:T(8,128)(2,1)}, u32[]{:S(2)}, u32[]{:S(2)}) collective-permute-start(bf16[512,1536]{1,0:T(8,128)(2,1)} %get-tuple-element.82), channel_id=1, source_target_pairs={{0,1},{1,0},{2,3},{3,2},{4,5},{5,4},{6,7},{7,6},{8,9},{9,8},{10,11... | collective-permute-start | bytes 4718600 | tf_op jit(solution)/shard_map/ppermute | solution.py:939
  163.3 8.7 %collective-permute-start.11 = (bf16[768,512]{1,0:T(8,128)(2,1)S(1)}, bf16[768,512]{1,0:T(8,128)(2,1)}, u32[]{:S(2)}, u32[]{:S(2)}) collective-permute-start(bf16[768,512]{1,0:T(8,128)(2,1)S(1)} %copy-done.38), channel_id=1, source_target_pairs={{0,1},{1,0},{2,3},{3,2},{4,5},{5,4},{6,7},{7,6},{8,9},{9,8},{10,11... | collective-permute-start | bytes 2359304 | tf_op jit(solution)/shard_map/ppermute | solution.py:939
  163.6 4.8 %collective-permute-start.13 = (bf16[512,384]{1,0:T(8,128)(2,1)}, bf16[512,384]{1,0:T(8,128)(2,1)S(1)}, u32[]{:S(2)}, u32[]{:S(2)}) collective-permute-start(bf16[512,384]{1,0:T(8,128)(2,1)} %get-tuple-element.86), channel_id=1, source_target_pairs={{0,1},{1,0},{2,3},{3,2},{4,5},{5,4},{6,7},{7,6},{8,9},{9,8},{10,11... | collective-permute-start | bytes 1179656 | tf_op jit(solution)/shard_map/ppermute | solution.py:939
  163.8 15.4 %collective-permute-start.10 = (bf16[512,384]{1,0:T(8,128)(2,1)}, bf16[512,384]{1,0:T(8,128)(2,1)}, u32[]{:S(2)}, u32[]{:S(2)}) collective-permute-start(bf16[512,384]{1,0:T(8,128)(2,1)} %get-tuple-element.78), channel_id=1, source_target_pairs={{0,1},{1,0},{2,3},{3,2},{4,5},{5,4},{6,7},{7,6},{8,9},{9,8},{10,11... | collective-permute-start | bytes 1179656 | tf_op jit(solution)/shard_map/ppermute | solution.py:939
  176.7 34.0 %collective-permute-start.17 = (bf16[8,48,768]{2,1,0:T(8,128)(2,1)S(1)}, bf16[8,48,768]{2,1,0:T(8,128)(2,1)S(1)}, u32[]{:S(2)}, u32[]{:S(2)}) collective-permute-start(bf16[8,48,768]{2,1,0:T(8,128)(2,1)S(1)} %dynamic-slice_bitcast_fusion.1.refs_0_), channel_id=1, source_target_pairs={{0,2},{1,3},{2,0},{3,1},{4,6},{5,7},{6,4},{7,5},{8,10},{9,11},{10,... | collective-permute-start | bytes 1769480 | tf_op jit(solution)/shard_map/ppermute | solution.py:944
  178.2 33.3 %collective-permute-start.18 = (bf16[8,48,768]{2,1,0:T(8,128)(2,1)S(1)}, bf16[8,48,768]{2,1,0:T(8,128)(2,1)S(1)}, u32[]{:S(2)}, u32[]{:S(2)}) collective-permute-start(bf16[8,48,768]{2,1,0:T(8,128)(2,1)S(1)} %bitcast.81), channel_id=1, source_target_pairs={{0,4},{1,5},{2,6},{3,7},{4,0},{5,1},{6,2},{7,3},{8,12},{9,13},{10,... | collective-permute-start | bytes 1769480 | tf_op jit(solution)/shard_map/ppermute | solution.py:944
  179.2 24.1 %copy-start.4 = (bf16[768,1024]{1,0:T(8,128)(2,1)S(1)}, bf16[768,1024]{1,0:T(8,128)(2,1)}, u32[]{:S(2)}) copy-start(bf16[768,1024]{1,0:T(8,128)(2,1)} %get-tuple-element.117.refs_0_.turned_ref) | copy-start | bytes 4718596
  179.3 24.1 %copy-start.48 = (f32[768,128]{1,0:T(8,128)S(1)}, f32[768,128]{1,0:T(8,128)}, u32[]{:S(2)}) copy-start(f32[768,128]{1,0:T(8,128)} %get-tuple-element.93.widen_ref) | copy-start | bytes 1179652
  179.3 24.1 %copy-start.53 = (f32[8,768]{1,0:T(8,128)S(1)}, f32[8,768]{1,0:T(8,128)}, u32[]{:S(2)}) copy-start(f32[8,768]{1,0:T(8,128)} %copy-done.52) | copy-start | bytes 73732
  179.3 24.1 %copy-start.54 = (f32[8,768]{1,0:T(8,128)S(1)}, f32[8,768]{1,0:T(8,128)}, u32[]{:S(2)}) copy-start(f32[8,768]{1,0:T(8,128)} %get-tuple-element.91.first_ref) | copy-start | bytes 73732
  206.1 6.3 %copy-start.6 = (bf16[1024,1152]{1,0:T(8,128)(2,1)S(1)}, bf16[1024,1152]{1,0:T(8,128)(2,1)}, u32[]{:S(2)}) copy-start(bf16[1024,1152]{1,0:T(8,128)(2,1)} %copy-done.5) | copy-start | bytes 7077892
  208.1 18.7 %collective-permute-start.16 = (bf16[8,48,896]{2,1,0:T(8,128)(2,1)}, bf16[8,48,896]{2,1,0:T(8,128)(2,1)}, u32[]{:S(2)}, u32[]{:S(2)}) collective-permute-start(bf16[8,48,896]{2,1,0:T(8,128)(2,1)} %bitcast.24.refs_1_.refs_11_), channel_id=1, source_target_pairs={{0,4},{1,5},{2,6},{3,7},{4,0},{5,1},{6,2},{7,3},{8,12},{9,13},{10,... | collective-permute-start | bytes 2064392 | tf_op jit(solution)/shard_map/ppermute | solution.py:944
  210.0 16.1 %collective-permute-start.15 = (bf16[8,48,768]{2,1,0:T(8,128)(2,1)}, bf16[8,48,768]{2,1,0:T(8,128)(2,1)}, u32[]{:S(2)}, u32[]{:S(2)}) collective-permute-start(bf16[8,48,768]{2,1,0:T(8,128)(2,1)} %dynamic-slice_bitcast_fusion.refs_0_.refs_10_), channel_id=1, source_target_pairs={{0,2},{1,3},{2,0},{3,1},{4,6},{5,7},{6,4},{7,5},{8,10},{9,11},{10,... | collective-permute-start | bytes 1769480 | tf_op jit(solution)/shard_map/ppermute | solution.py:944
  220.5 13.7 %collective-permute-start.21 = (bf16[4,48,768]{2,1,0:T(8,128)(2,1)}, bf16[4,48,768]{2,1,0:T(8,128)(2,1)S(1)}, u32[]{:S(2)}, u32[]{:S(2)}) collective-permute-start(bf16[4,48,768]{2,1,0:T(8,128)(2,1)} %get-tuple-element.98.refs_8_), channel_id=1, source_target_pairs={{0,4},{1,5},{2,6},{3,7},{4,0},{5,1},{6,2},{7,3},{8,12},{9,13},{10,... | collective-permute-start | bytes 884744 | tf_op jit(solution)/shard_map/ppermute | solution.py:944
  222.0 12.2 %collective-permute-start.22 = (bf16[4,48,768]{2,1,0:T(8,128)(2,1)}, bf16[4,48,768]{2,1,0:T(8,128)(2,1)S(1)}, u32[]{:S(2)}, u32[]{:S(2)}) collective-permute-start(bf16[4,48,768]{2,1,0:T(8,128)(2,1)} %get-tuple-element.99.refs_9_), channel_id=1, source_target_pairs={{0,2},{1,3},{2,0},{3,1},{4,6},{5,7},{6,4},{7,5},{8,10},{9,11},{10,... | collective-permute-start | bytes 884744 | tf_op jit(solution)/shard_map/ppermute | solution.py:944
  232.5 7.9 %collective-permute-start.20 = (bf16[4,48,896]{2,1,0:T(8,128)(2,1)S(1)}, bf16[4,48,896]{2,1,0:T(8,128)(2,1)S(1)}, u32[]{:S(2)}, u32[]{:S(2)}) collective-permute-start(bf16[4,48,896]{2,1,0:T(8,128)(2,1)S(1)} %get-tuple-element.103.refs_9_), channel_id=1, source_target_pairs={{0,2},{1,3},{2,0},{3,1},{4,6},{5,7},{6,4},{7,5},{8,10},{9,11},{10,... | collective-permute-start | bytes 1032200 | tf_op jit(solution)/shard_map/ppermute | solution.py:944
  233.6 6.7 %collective-permute-start.19 = (bf16[4,48,768]{2,1,0:T(8,128)(2,1)S(1)}, bf16[4,48,768]{2,1,0:T(8,128)(2,1)S(1)}, u32[]{:S(2)}, u32[]{:S(2)}) collective-permute-start(bf16[4,48,768]{2,1,0:T(8,128)(2,1)S(1)} %get-tuple-element.101.refs_8_), channel_id=1, source_target_pairs={{0,4},{1,5},{2,6},{3,7},{4,0},{5,1},{6,2},{7,3},{8,12},{9,13},{10,... | collective-permute-start | bytes 884744 | tf_op jit(solution)/shard_map/ppermute | solution.py:944
  234.9 12.2 %collective-permute-start.24 = (bf16[2,48,1536]{2,1,0:T(8,128)(2,1)S(1)}, bf16[2,48,1536]{2,1,0:T(8,128)(2,1)S(1)}, u32[]{:S(2)}, u32[]{:S(2)}) collective-permute-start(bf16[2,48,1536]{2,1,0:T(8,128)(2,1)S(1)} %get-tuple-element.106.refs_8_), channel_id=1, source_target_pairs={{0,8},{1,9},{2,10},{3,11},{4,12},{5,13},{6,14},{7,15},{8,0},{9,1},... | collective-permute-start | bytes 884744 | tf_op jit(solution)/shard_map/ppermute | solution.py:944
  241.1 14.9 %collective-permute-start.23 = (bf16[2,48,1664]{2,1,0:T(8,128)(2,1)S(1)}, bf16[2,48,1664]{2,1,0:T(8,128)(2,1)S(1)}, u32[]{:S(2)}, u32[]{:S(2)}) collective-permute-start(bf16[2,48,1664]{2,1,0:T(8,128)(2,1)S(1)} %get-tuple-element.108.refs_4_), channel_id=1, source_target_pairs={{0,8},{1,9},{2,10},{3,11},{4,12},{5,13},{6,14},{7,15},{8,0},{9,1},... | collective-permute-start | bytes 958472 | tf_op jit(solution)/shard_map/ppermute | solution.py:944
  247.7 9.4 %collective-permute-start.27 = (bf16[1,48,1536]{2,1,0:T(8,128)(2,1)S(1)}, bf16[1,48,1536]{2,1,0:T(8,128)(2,1)S(1)}, u32[]{:S(2)}, u32[]{:S(2)}) collective-permute-start(bf16[1,48,1536]{2,1,0:T(8,128)(2,1)S(1)} %get-tuple-element.110.refs_4_), channel_id=1, source_target_pairs={{0,16},{1,17},{2,18},{3,19},{4,20},{5,21},{6,22},{7,23},{8,24},{9,... | collective-permute-start | bytes 442376 | tf_op jit(solution)/shard_map/ppermute | solution.py:944
  256.6 10.1 %collective-permute-start.25 = (bf16[1,48,1664]{2,1,0:T(8,128)(2,1)S(1)}, bf16[1,48,1664]{2,1,0:T(8,128)(2,1)}, u32[]{:S(2)}, u32[]{:S(2)}) collective-permute-start(bf16[1,48,1664]{2,1,0:T(8,128)(2,1)S(1)} %get-tuple-element.112), channel_id=1, source_target_pairs={{0,16},{1,17},{2,18},{3,19},{4,20},{5,21},{6,22},{7,23},{8,24},{9,... | collective-permute-start | bytes 479240 | tf_op jit(solution)/shard_map/ppermute | solution.py:944
  257.1 10.8 %collective-permute-start.28 = (f32[48,1536]{1,0:T(8,128)S(1)}, f32[48,1536]{1,0:T(8,128)S(1)}, u32[]{:S(2)}, u32[]{:S(2)}) collective-permute-start(f32[48,1536]{1,0:T(8,128)S(1)} %add_bitcast_fusion.2), channel_id=1, source_target_pairs={{0,1},{1,0},{2,3},{3,2},{4,5},{5,4},{6,7},{7,6},{8,9},{9,8},{10,11... | collective-permute-start | bytes 884744 | tf_op jit(solution)/shard_map/ppermute | solution.py:939
  266.2 6.6 %collective-permute-start.14 = (f32[512,768]{1,0:T(8,128)}, f32[512,768]{1,0:T(8,128)}, u32[]{:S(2)}, u32[]{:S(2)}) collective-permute-start(f32[512,768]{1,0:T(8,128)} %get-tuple-element.97), channel_id=1, source_target_pairs={{0,1},{1,0},{2,3},{3,2},{4,5},{5,4},{6,7},{7,6},{8,9},{9,8},{10,11... | collective-permute-start | bytes 4718600 | tf_op jit(solution)/shard_map/ppermute | solution.py:939
  267.7 3.0 %collective-permute-start.26 = (f32[48,1664]{1,0:T(8,128)S(1)}, f32[48,1664]{1,0:T(8,128)S(1)}, u32[]{:S(2)}, u32[]{:S(2)}) collective-permute-start(f32[48,1664]{1,0:T(8,128)S(1)} %add_bitcast_fusion.1.own_ref), channel_id=1, source_target_pairs={{0,1},{1,0},{2,3},{3,2},{4,5},{5,4},{6,7},{7,6},{8,9},{9,8},{10,11... | collective-permute-start | bytes 958472 | tf_op jit(solution)/shard_map/ppermute | solution.py:939
  268.0 2.6 collective-permute-start.29
  (44 other events, 83.7 us)
Sparse Core Ops, SparseCore 0:
  11.5 101.7 all-gather.1
  145.6 36.3 reduce-scatter.6
  223.1 22.7 reduce-scatter.4

commit v2 on v1

--- a/solution.py
+++ b/solution.py
@@ -876,11 +876,9 @@
     )(place, inputs, left, left_other, right, right_other)
 
 
-def pack_kernel(core_ref, narrow_ref, mixing_ref, widen_ref, project_ref, biases_ref, norms_ref, hidden_ref,
-                rest_ref, packed_ref):
+def pack_rest_kernel(core_ref, narrow_ref, mixing_ref, widen_ref, rest_ref):
     core = core_ref[0]
     shard, width = mixing_ref.shape
-    half = width // 2
     split = rest_ref.shape[0] - narrow_ref.shape[0]
     blocks = widen_ref.shape[1] // width
 
@@ -899,8 +897,29 @@
         if at < rest_ref.shape[0]:
             rest_ref[at:] = jnp.zeros((rest_ref.shape[0] - at, width), jnp.bfloat16)
 
+
+def pack_rest(core, narrowing, mixing, widening):
+    shard, width = mixing.shape
+    rows = narrowing.shape[0] + shard + widening.shape[1] // width * shard
+    half_rows = -(-rows // 32) * 16
+    whole = pl.BlockSpec(memory_space=pltpu.VMEM)
+    return pl.pallas_call(
+        pack_rest_kernel,
+        in_specs=[pl.BlockSpec(memory_space=pltpu.SMEM)] + [whole] * 3,
+        out_specs=whole,
+        out_shape=jax.ShapeDtypeStruct((half_rows, width), jnp.bfloat16),
+        compiler_params=pltpu.CompilerParams(vmem_limit_bytes=60 * 2**20),
+        cost_estimate=cost(2.0),
+        name="pack_rest",
+    )(core, narrowing, mixing, widening)
+
+
+def pack_kernel(core_ref, project_ref, biases_ref, norms_ref, hidden_ref, packed_ref):
+    core = core_ref[0]
+    shard = packed_ref.shape[0]
+    half = project_ref.shape[1] // 6
     for kind in range(3):
-        from_ = pl.ds(pl.multiple_of(core * half + kind * width, half), half)
+        from_ = pl.ds(pl.multiple_of(core * half + kind * 2 * half, half), half)
         packed_ref[:, kind * half : (kind + 1) * half] = project_ref[:, from_]
     place = lax.broadcasted_iota(jnp.int32, (128, shard), 0)
     total = jnp.zeros((128, shard), jnp.float32)
@@ -912,23 +931,18 @@
     packed_ref[:, 3 * half :] = total.T.astype(jnp.bfloat16)
 
 
-def pack(core, narrowing, mixing, widening, projection, biases, norms, hidden):
-    shard, width = mixing.shape
-    rows = narrowing.shape[0] + shard + widening.shape[1] // width * shard
-    half_rows = -(-rows // 32) * 16
+def pack(core, projection, biases, norms, hidden):
+    shard = projection.shape[0]
     whole = pl.BlockSpec(memory_space=pltpu.VMEM)
     return pl.pallas_call(
         pack_kernel,
-        in_specs=[pl.BlockSpec(memory_space=pltpu.SMEM)] + [whole] * 7,
-        out_specs=[whole] * 2,
-        out_shape=[
-            jax.ShapeDtypeStruct((half_rows, width), jnp.bfloat16),
-            jax.ShapeDtypeStruct((shard, projection.shape[1] // 2 + 128), jnp.bfloat16),
-        ],
+        in_specs=[pl.BlockSpec(memory_space=pltpu.SMEM)] + [whole] * 4,
+        out_specs=whole,
+        out_shape=jax.ShapeDtypeStruct((shard, projection.shape[1] // 2 + 128), jnp.bfloat16),
         compiler_params=pltpu.CompilerParams(vmem_limit_bytes=60 * 2**20),
         cost_estimate=cost(2.0),
         name="pack",
-    )(core, narrowing, mixing, widening, projection, biases, norms, hidden)
+    )(core, projection, biases, norms, hidden)
 
 
 AXES = ("fsdp", "ctx")
@@ -1123,7 +1137,8 @@
     swap = lambda value: core_permute(value, chips)
 
     hidden = widen_bias.shape[0] // shard
-    rest, packed = pack(core_at, narrowing, mixing, widening, projection, biases, norms, widen_bias.reshape(hidden, shard))
+    rest = pack_rest(core_at, narrowing, mixing, widening)
+    packed = pack(core_at, projection, biases, norms, widen_bias.reshape(hidden, shard))
     rest = lax.all_gather(rest, AXES, axis=0, tiled=True).reshape(chips, -1, model_width)
     packed = packed.reshape([1] * len(bits) + [shard, packed.shape[1]])
     cut = packed.shape[-1] // 2
@@ -1202,7 +1217,7 @@
     other_share = swap(last_share)
 
     grad_projection, grad_mixing, small_share = finish(
-        core_at, last_share, other_share, half, [widen_share, narrow_share]
+        core_at, last_share, other_share, half, [widen_share, narrow_share, input_grad]
     )
     return (
         result.astype(jnp.bfloat16)[None],

time: 283 us -> 278 us (0.982)
    unnamed x119 -> x117, local copies, waits for them, and re-layouts: 33.9 us -> 34.6 us
where the time goes in v2:
time: 278 us; the launch traced here: 277 us
  Pallas kernels  107 us (38%)
  waiting for transfers between devices  80.1 us (29%)
  local copies, waits for them, and re-layouts  41.9 us (15%)
  starting transfers between devices  25.5 us (9%)
  between operations  15 us (5%)
  other arithmetic  7.32 us (3%)
    ppermute x18, waiting for transfers between devices, chip_permute(): return lax.ppermute(value, AXES, pairs)  55 us
    unnamed x117, local copies, waits for them, and re-layouts  34.6 us
    pallas_call x1, Pallas kernels, attn_bwd(): pl.pallas_call(attn_bwd_kernel, grid_spec=pltpu.PrefetchScalarGridSpec(nu...  24 us
    ppermute x18, starting transfers between devices, chip_permute(): return lax.ppermute(value, AXES, pairs)  22.4 us
    pallas_call x1, Pallas kernels, back(): pl.pallas_call(functools.partial(back_kernel, spare=len(before)), grid_sp...  17.4 us
    pallas_call x1, Pallas kernels, attn_fwd(): pl.pallas_call(attn_fwd_kernel, grid=(pairs, L // QB), in_specs=[pl.Block...  15 us
    all_gather x1, waiting for transfers between devices, fast_body(): lax.all_gather(rest, AXES, axis=0, tiled=True)  14.7 us
    pallas_call x1, Pallas kernels, widen(): pl.pallas_call(widen_kernel, grid_spec=pltpu.PrefetchScalarGridSpec(num_s...  10.8 us
  transfers between devices with their start and end apart: 33, of which 16 were waited for; matrix products, arithmetic and copies ran while one was open for 5% of the time, Pallas kernels for 32%

profile of v2, /device:TPU:0, one launch (start us, length us, event | category | flops | bytes accessed | tf_op | source)
XLA Modules:
  0.0 276.8 jit_solution(1082578422894259484)
XLA Ops:
  7.2 1.8 pack_rest.1
  9.2 1.3 reshape.89.hidden_ref
  10.5 1.7 pack.1
  12.1 4.0 %collective-permute-start.1 = (bf16[1,1,1,1,48,1280]{5,4,3,2,1,0:T(8,128)(2,1)}, bf16[1,1,1,1,48,1280]{5,4,3,2,1,0:T(8,128)(2,1)S(1)}, u32[]{:S(2)}, u32[]{:S(2)}) collective-permute-start(bf16[1,1,1,1,48,1280]{5,4,3,2,1,0:T(8,128)(2,1)} %bitcast.89), channel_id=1, source_target_pairs={{0,16},{1,17},{2,18},{3,19},{4,20},{5,21},{6,22},{7,23},{8,24},{9,... | collective-permute-start | bytes 368648 | tf_op jit(solution)/shard_map/ppermute | solution.py:958
  16.2 6.2 %collective-permute-done.1 = bf16[1,1,1,1,48,1280]{5,4,3,2,1,0:T(8,128)(2,1)S(1)} collective-permute-done((bf16[1,1,1,1,48,1280]{5,4,3,2,1,0:T(8,128)(2,1)}, bf16[1,1,1,1,48,1280]{5,4,3,2,1,0:T(8,128)(2,1)S(1)}, u32[]{:S(2)}, u32[]{:S(2)}) %collective-permute-start.1) | collective-permute-done | bytes 122912 | tf_op jit(solution)/shard_map/ppermute | solution.py:958
  24.2 11.7 %collective-permute-done.2 = bf16[2,1,1,1,48,1280]{5,4,3,2,1,0:T(8,128)(2,1)S(1)} collective-permute-done((bf16[2,1,1,1,48,1280]{5,4,3,2,1,0:T(8,128)(2,1)S(1)}, bf16[2,1,1,1,48,1280]{5,4,3,2,1,0:T(8,128)(2,1)S(1)}, u32[]{:S(2)}, u32[]{:S(2)}) %collective-permute-start.2) | collective-permute-done | bytes 245792 | tf_op jit(solution)/shard_map/ppermute | solution.py:958
  36.0 1.3 collective-permute-start.3
  39.2 1.5 collective-permute-start.5
  40.8 2.3 collective-permute-done.3
  44.1 4.7 %collective-permute-done.5 = bf16[2,2,1,1,48,640]{5,4,3,2,1,0:T(8,128)(2,1)S(1)} collective-permute-done((bf16[2,2,1,1,48,640]{5,4,3,2,1,0:T(8,128)(2,1)S(1)}, bf16[2,2,1,1,48,640]{5,4,3,2,1,0:T(8,128)(2,1)S(1)}, u32[]{:S(2)}, u32[]{:S(2)}) %collective-permute-start.5) | collective-permute-done | bytes 245792 | tf_op jit(solution)/shard_map/ppermute | solution.py:958
  49.0 1.6 broadcast_select_fusion.1
  50.6 2.1 fusion.1
  52.7 2.6 copy.28.x_ref
  55.3 7.7 %collective-permute-done.4 = bf16[2,2,1,2,48,640]{5,4,3,2,1,0:T(8,128)(2,1)S(1)} collective-permute-done((bf16[2,2,1,2,48,640]{5,4,3,2,1,0:T(8,128)(2,1)S(1)}, bf16[2,2,1,2,48,640]{5,4,3,2,1,0:T(8,128)(2,1)S(1)}, u32[]{:S(2)}, u32[]{:S(2)}) %collective-permute-start.4) | collective-permute-done | bytes 491552 | tf_op jit(solution)/shard_map/ppermute | solution.py:958
  63.8 3.8 %collective-permute-done.6 = bf16[2,2,2,1,48,640]{5,4,3,2,1,0:T(8,128)(2,1)S(1)} collective-permute-done((bf16[2,2,2,1,48,640]{5,4,3,2,1,0:T(8,128)(2,1)S(1)}, bf16[2,2,2,1,48,640]{5,4,3,2,1,0:T(8,128)(2,1)S(1)}, u32[]{:S(2)}, u32[]{:S(2)}) %collective-permute-start.6) | collective-permute-done | bytes 491552 | tf_op jit(solution)/shard_map/ppermute | solution.py:958
  68.4 1.4 copy-done.16
  74.0 2.9 %qkv.1 = (bf16[1024,1152]{1,0:T(8,128)(2,1)S(1)}, bf16[768,1152]{1,0:T(8,128)(2,1)S(1)}, f32[16,768]{1,0:T(8,128)S(1)}) custom-call(s32[5]{0:T(128)S(1)} %concatenate.25.place_ref, bf16[1024,768]{1,0:T(8,128)(2,1)S(1)} %copy-done.16, bf16[4,2,48,640]{3,2,1,0:T(8,128)(2,1)S(1)} %bitcast.83, bf16[4,2,48,640]{3,2,1,0:T(8,128)(2,1)S(1)} %bitcast.86, ...), custom_call_target="tpu_custom_call" | custom-call | flops 200000000 | bytes 4096 | tf_op jit(solution)/shard_map/qkv/pallas_call | solution.py:863
  78.2 15.0 %attn_fwd.1 = (bf16[1024,384]{1,0:T(8,128)(2,1)}, f32[3,2,1024]{2,1,0:T(2,128)S(1)}) custom-call(s32[1]{0:T(128)S(6)} %copy.42.len_ref, bf16[1024,1152]{1,0:T(8,128)(2,1)S(1)} %get-tuple-element.61.q_ref.k_ref.v_ref, bf16[1024,1152]{1,0:T(8,128)(2,1)S(1)} %get-tuple-element.61.q_ref.k_ref.v_ref, bf16[1024,1152]{1,0:T(8,128)(2,1)S(1)} %get-tuple-element.61.q_ref.k_ref.v_ref, ...), custom_call_target="tpu_custom_call" | custom-call | flops 725000000 | bytes 4096 | tf_op jit(solution)/shard_map/attn_fwd/pallas_call | solution.py:235
  94.0 2.4 collective-permute-done.7.other_ref
  96.4 14.7 %all-gather.2.cloned.1.call-done = bf16[7168,768]{1,0:T(8,128)(2,1)} async-done(((bf16[224,768]{1,0:T(8,128)(2,1)}), bf16[7168,768]{1,0:T(8,128)(2,1)}) %all-gather.2.cloned.1.call-update) | async-done | bytes 11010064 | tf_op jit(solution)/shard_map/all_gather | solution.py:1142
  111.1 4.1 %copy-done = bf16[7168,768]{1,0:T(8,128)(2,1)S(1)} copy-done((bf16[7168,768]{1,0:T(8,128)(2,1)S(1)}, bf16[7168,768]{1,0:T(8,128)(2,1)}, u32[]{:S(2)}) %copy-start) | copy-done | bytes 11010072
  115.2 10.8 %widen.1 = (bf16[512,768]{1,0:T(8,128)(2,1)}, bf16[768,512]{1,0:T(8,128)(2,1)S(1)}, f32[512,768]{1,0:T(8,128)S(1)}, f32[512,1]{1,0:T(8,128)S(1)}, bf16[512,3072]...) custom-call(s32[1]{0:T(128)} %bitcast.core_ref, bf16[1024,384]{1,0:T(8,128)(2,1)} %get-tuple-element.62.own_ref, ...), custom_call_target="tpu_custom_call" | custom-call | flops 625000000 | bytes 4096 | tf_op jit(solution)/shard_map/widen/pallas_call | solution.py:391
  126.4 6.3 %narrow.1 = (bf16[512,768]{1,0:T(8,128)(2,1)}, f32[512,768]{1,0:T(8,128)S(1)}, bf16[512,768]{1,0:T(8,128)(2,1)S(1)}, bf16[512,384]{1,0:T(8,128)(2,1)S(1)}, bf16[...) custom-call(s32[1]{0:T(128)} %bitcast.core_ref, bf16[512,3072]{1,0:T(8,128)(2,1)S(1)} %get-tuple-element.64.g_ref.own_ref, ...), custom_call_target="tpu_custom_call" | custom-call | flops 400000000 | bytes 4096 | tf_op jit(solution)/shard_map/narrow/pallas_call | solution.py:742
  135.7 1.5 collective-permute-done.9.dm_other_ref
  137.1 4.7 %narrow_grad.1.refs_0_ = bf16[4,4,192,384]{3,2,1,0:T(8,128)(2,1)S(1)} custom-call(bf16[512,3072]{1,0:T(8,128)(2,1)S(1)} %get-tuple-element.64.g_ref.own_ref, bf16[512,3072]{1,0:T(8,128)(2,1)S(1)} %collective-permute-done.8.other_ref, bf16[512,384]{1,0:T(8,128)(2,1)S(1)} %get-tuple-element.71.dm_own_ref, bf16[512,384]{1,0:T(8,128)(2,1)S(1)} %collective-permute-done.9.dm_other_ref), custom_call_target="tpu_custom_call" | custom-call | flops 225000000 | bytes 4096 | tf_op jit(solution)/shard_map/narrow_grad/pallas_call | solution.py:789
  141.8 1.4 copy-done.2
  143.3 17.4 %back.1 = (bf16[512,1536]{1,0:T(8,128)(2,1)}, bf16[512,1536]{1,0:T(8,128)(2,1)}, f32[768,128]{1,0:T(8,128)}, f32[512,768]{1,0:T(8,128)}, bf16[512,768]{1,0:T(8,1...) custom-call(s32[1]{0:T(128)} %bitcast.core_ref, ...), custom_call_target="tpu_custom_call" | custom-call | flops 690000000 | bytes 4096 | tf_op jit(solution)/shard_map/back/pallas_call | solution.py:501
  161.9 4.3 %collective-permute-done.13.grad_other_ref = bf16[512,384]{1,0:T(8,128)(2,1)S(1)} collective-permute-done((bf16[512,384]{1,0:T(8,128)(2,1)}, bf16[512,384]{1,0:T(8,128)(2,1)S(1)}, u32[]{:S(2)}, u32[]{:S(2)}) %collective-permute-start.13) | collective-permute-done | bytes 393248 | tf_op jit(solution)/shard_map/ppermute | solution.py:953
  167.3 2.5 mixing_grad.1.refs_2_.mixing_ref
  169.9 4.5 %widen_grad.1 = (bf16[768,768]{1,0:T(8,128)(2,1)S(1)}, bf16[768,768]{1,0:T(8,128)(2,1)S(1)}) custom-call(bf16[768,512]{1,0:T(8,128)(2,1)S(1)} %copy-done.38, bf16[768,512]{1,0:T(8,128)(2,1)} %collective-permute-done.11.other_ref, bf16[512,1536]{1,0:T(8,128)(2,1)S(1)} %copy-done.34, bf16[512,1536]{1,0:T(8,128)(2,1)} %collective-permute-done.12.grad_other_ref), custom_call_target="tpu_custom_call" | custom-call | flops 200000000 | bytes 4096 | tf_op jit(solution)/shard_map/widen_grad/pallas_call | solution.py:609
  174.4 1.5 collective-permute-start.17
  177.0 24.0 %attn_bwd.1 = (bf16[1024,1152]{1,0:T(8,128)(2,1)S(1)}, f32[8,1152]{1,0:T(8,128)S(1)}) custom-call(s32[1]{0:T(128)} %bitcast.core_ref, s32[1]{0:T(128)S(6)} %copy.42.len_ref, bf16[1024,1152]{1,0:T(8,128)(2,1)S(1)} %get-tuple-element.61.q_ref.k_ref.v_ref, bf16[1024,1152]{1,0:T(8,128)(2,1)S(1)} %get-tuple-element.61.q_ref.k_ref.v_ref, ...), custom_call_target="tpu_custom_call" | custom-call | flops 1100000000 | bytes 4096 | tf_op jit(solution)/shard_map/attn_bwd/pallas_call | solution.py:307
  201.1 2.7 last_grad.1
  214.6 2.0 hop.6
  218.3 1.5 collective-permute-start.21
  220.7 3.1 %collective-permute-done.15.refs_1_.refs_3_ = bf16[8,48,768]{2,1,0:T(8,128)(2,1)} collective-permute-done((bf16[8,48,768]{2,1,0:T(8,128)(2,1)}, bf16[8,48,768]{2,1,0:T(8,128)(2,1)}, u32[]{:S(2)}, u32[]{:S(2)}) %collective-permute-start.15) | collective-permute-done | bytes 589856 | tf_op jit(solution)/shard_map/ppermute | solution.py:958
  224.5 1.4 copy-done.8
  227.2 3.0 %hop.7 = (bf16[4,48,768]{2,1,0:T(8,128)(2,1)S(1)}, f32[4,48,768]{2,1,0:T(8,128)S(1)}, bf16[4,48,896]{2,1,0:T(8,128)(2,1)S(1)}, f32[4,48,896]{2,1,0:T(8,128)S(1)}) custom-call(s32[4]{0:T(128)S(1)} %pad_add_fusion.bits_ref, bf16[16,48,768]{2,1,0:T(8,128)(2,1)S(1)} %bitcast.75, bf16[8,48,768]{2,1,0:T(8,128)(2,1)} %collective-permute-done.15.refs_1_.refs_3_, ...), custom_call_target="tpu_custom_call" | custom-call | flops 100000000 | bytes 4096 | tf_op jit(solution)/shard_map/hop/pallas_call | solution.py:1051
  232.7 1.3 collective-permute-start.24
  234.0 4.1 %collective-permute-done.19.refs_1_.refs_3_ = bf16[4,48,768]{2,1,0:T(8,128)(2,1)S(1)} collective-permute-done((bf16[4,48,768]{2,1,0:T(8,128)(2,1)S(1)}, bf16[4,48,768]{2,1,0:T(8,128)(2,1)S(1)}, u32[]{:S(2)}, u32[]{:S(2)}) %collective-permute-start.19) | collective-permute-done | bytes 294944 | tf_op jit(solution)/shard_map/ppermute | solution.py:958
  238.8 1.3 collective-permute-start.23
  240.1 4.7 %collective-permute-done.24.refs_1_.refs_3_ = bf16[2,48,1536]{2,1,0:T(8,128)(2,1)S(1)} collective-permute-done((bf16[2,48,1536]{2,1,0:T(8,128)(2,1)S(1)}, bf16[2,48,1536]{2,1,0:T(8,128)(2,1)S(1)}, u32[]{:S(2)}, u32[]{:S(2)}) %collective-permute-start.24) | collective-permute-done | bytes 294944 | tf_op jit(solution)/shard_map/ppermute | solution.py:958
  245.5 2.2 collective-permute-start.27
  247.7 6.0 %collective-permute-done.23.refs_1_.refs_3_ = bf16[2,48,1664]{2,1,0:T(8,128)(2,1)S(1)} collective-permute-done((bf16[2,48,1664]{2,1,0:T(8,128)(2,1)S(1)}, bf16[2,48,1664]{2,1,0:T(8,128)(2,1)S(1)}, u32[]{:S(2)}, u32[]{:S(2)}) %collective-permute-start.23) | collective-permute-done | bytes 319520 | tf_op jit(solution)/shard_map/ppermute | solution.py:958
  255.9 1.5 copy-done.55
  257.4 1.4 copy-done.56
  258.8 4.0 %tokens_grad.1 = (f32[512,768]{1,0:T(8,128)S(1)}, f32[512,768]{1,0:T(8,128)S(1)}) custom-call(s32[1]{0:T(128)} %bitcast.core_ref, bf16[1024,1152]{1,0:T(8,128)(2,1)S(1)} %copy-done.6, bf16[768,1152]{1,0:T(8,128)(2,1)S(1)} %copy-done.55, f32[512,768]{1,0:T(8,128)S(1)} %copy-done.56, bf16[8,48,768]{2,1,0:T(8,128)(2,1)} %dynamic-slice_bitcast_fusion.refs_0_.refs_10_, ...), custom_call_target="tpu_custom_call" | custom-call | flops 5000000000 | bytes 4096 | tf_op jit(solution)/shard_map/tokens_grad/pallas_call | solution.py:573
  265.1 2.2 collective-permute-done.29
  (190 shorter events, 45.6 us)
Async XLA Ops:
  7.2 103.9 %all-gather.2.cloned.1.call-start = ((), (), s32[]{:S(2)}) async-start(), calls=%async_computation.2 | async-start | bytes 11354112 | tf_op jit(solution)/shard_map/all_gather | solution.py:1142
  9.1 201.0 %reduce-scatter.7.cloned.1.call-start = ((), (), s32[]{:S(2)}) async-start(), calls=%async_computation.4 | async-start | bytes 2949120
  12.1 25.2 %copy-start.17 = (bf16[1,512,768]{2,1,0:T(8,128)(2,1)S(1)}, bf16[1,512,768]{2,1,0:T(8,128)(2,1)}, u32[]{:S(2)}) copy-start(bf16[1,512,768]{2,1,0:T(8,128)(2,1)} %param.10) | copy-start | bytes 2359300
  12.1 10.2 %collective-permute-start.1 = (bf16[1,1,1,1,48,1280]{5,4,3,2,1,0:T(8,128)(2,1)}, bf16[1,1,1,1,48,1280]{5,4,3,2,1,0:T(8,128)(2,1)S(1)}, u32[]{:S(2)}, u32[]{:S(2)}) collective-permute-start(bf16[1,1,1,1,48,1280]{5,4,3,2,1,0:T(8,128)(2,1)} %bitcast.89), channel_id=1, source_target_pairs={{0,16},{1,17},{2,18},{3,19},{4,20},{5,21},{6,22},{7,23},{8,24},{9,... | collective-permute-start | bytes 368648 | tf_op jit(solution)/shard_map/ppermute | solution.py:958
  23.3 12.6 %collective-permute-start.2 = (bf16[2,1,1,1,48,1280]{5,4,3,2,1,0:T(8,128)(2,1)S(1)}, bf16[2,1,1,1,48,1280]{5,4,3,2,1,0:T(8,128)(2,1)S(1)}, u32[]{:S(2)}, u32[]{:S(2)}) collective-permute-start(bf16[2,1,1,1,48,1280]{5,4,3,2,1,0:T(8,128)(2,1)S(1)} %pad_maximum_fusion.6), channel_id=1, source_target_pairs={{0,8},{1,9},{2,10},{3,11},{4,12},{5,13},{6,14},{7,15},{8,0},{9,1},... | collective-permute-start | bytes 737288 | tf_op jit(solution)/shard_map/ppermute | solution.py:958
  36.0 7.0 %collective-permute-start.3 = (bf16[2,2,1,1,48,640]{5,4,3,2,1,0:T(8,128)(2,1)S(1)}, bf16[2,2,1,1,48,640]{5,4,3,2,1,0:T(8,128)(2,1)S(1)}, u32[]{:S(2)}, u32[]{:S(2)}) collective-permute-start(bf16[2,2,1,1,48,640]{5,4,3,2,1,0:T(8,128)(2,1)S(1)} %get-tuple-element.122), channel_id=1, source_target_pairs={{0,2},{1,3},{2,0},{3,1},{4,6},{5,7},{6,4},{7,5},{8,10},{9,11},{10,... | collective-permute-start | bytes 737288 | tf_op jit(solution)/shard_map/ppermute | solution.py:958
  38.5 10.6 %collective-permute-start = (bf16[512,768]{0,1:T(8,128)(2,1)}, bf16[512,768]{0,1:T(8,128)(2,1)}, u32[]{:S(2)}, u32[]{:S(2)}) collective-permute-start(bf16[512,768]{0,1:T(8,128)(2,1)} %bitcast.5), channel_id=1, source_target_pairs={{0,1},{1,0},{2,3},{3,2},{4,5},{5,4},{6,7},{7,6},{8,9},{9,8},{10,11... | collective-permute-start | bytes 2359304 | tf_op jit(solution)/shard_map/ppermute | solution.py:953
  39.2 9.6 %collective-permute-start.5 = (bf16[2,2,1,1,48,640]{5,4,3,2,1,0:T(8,128)(2,1)S(1)}, bf16[2,2,1,1,48,640]{5,4,3,2,1,0:T(8,128)(2,1)S(1)}, u32[]{:S(2)}, u32[]{:S(2)}) collective-permute-start(bf16[2,2,1,1,48,640]{5,4,3,2,1,0:T(8,128)(2,1)S(1)} %get-tuple-element.121), channel_id=1, source_target_pairs={{0,4},{1,5},{2,6},{3,7},{4,0},{5,1},{6,2},{7,3},{8,12},{9,13},{10,... | collective-permute-start | bytes 737288 | tf_op jit(solution)/shard_map/ppermute | solution.py:958
  43.1 7.5 %copy-start.29 = (bf16[2,2,1,2,48,640]{5,4,3,2,1,0:T(8,128)(2,1)}, bf16[2,2,1,2,48,640]{5,4,3,2,1,0:T(8,128)(2,1)S(1)}, u32[]{:S(2)}) copy-start(bf16[2,2,1,2,48,640]{5,4,3,2,1,0:T(8,128)(2,1)S(1)} %pad_maximum_fusion.3) | copy-start | bytes 1474564
  43.2 19.9 %collective-permute-start.4 = (bf16[2,2,1,2,48,640]{5,4,3,2,1,0:T(8,128)(2,1)S(1)}, bf16[2,2,1,2,48,640]{5,4,3,2,1,0:T(8,128)(2,1)S(1)}, u32[]{:S(2)}, u32[]{:S(2)}) collective-permute-start(bf16[2,2,1,2,48,640]{5,4,3,2,1,0:T(8,128)(2,1)S(1)} %pad_maximum_fusion.3), channel_id=1, source_target_pairs={{0,4},{1,5},{2,6},{3,7},{4,0},{5,1},{6,2},{7,3},{8,12},{9,13},{10,... | collective-permute-start | bytes 1474568 | tf_op jit(solution)/shard_map/ppermute | solution.py:958
  49.0 18.7 %collective-permute-start.6 = (bf16[2,2,2,1,48,640]{5,4,3,2,1,0:T(8,128)(2,1)S(1)}, bf16[2,2,2,1,48,640]{5,4,3,2,1,0:T(8,128)(2,1)S(1)}, u32[]{:S(2)}, u32[]{:S(2)}) collective-permute-start(bf16[2,2,2,1,48,640]{5,4,3,2,1,0:T(8,128)(2,1)S(1)} %pad_maximum_fusion.4), channel_id=1, source_target_pairs={{0,2},{1,3},{2,0},{3,1},{4,6},{5,7},{6,4},{7,5},{8,10},{9,11},{10,... | collective-permute-start | bytes 1474568 | tf_op jit(solution)/shard_map/ppermute | solution.py:958
  78.2 48.2 %copy-start.42 = (f32[16,768]{1,0:T(8,128)}, f32[16,768]{1,0:T(8,128)S(1)}, u32[]{:S(2)}) copy-start(f32[16,768]{1,0:T(8,128)S(1)} %get-tuple-element.63.rows_ref) | copy-start | bytes 147460
  93.8 2.6 collective-permute-start.7
  115.2 11.2 %copy-start.1 = (bf16[7168,768]{1,0:T(8,128)(2,1)S(1)}, bf16[7168,768]{1,0:T(8,128)(2,1)}, u32[]{:S(2)}) copy-start(bf16[7168,768]{1,0:T(8,128)(2,1)} %all-gather.2.cloned.1.call-done) | copy-start | bytes 33030148
  115.2 11.2 %copy-start.35 = (bf16[1,512,768]{2,1,0:T(8,128)(2,1)S(1)}, bf16[1,512,768]{2,1,0:T(8,128)(2,1)}, u32[]{:S(2)}) copy-start(bf16[1,512,768]{2,1,0:T(8,128)(2,1)} %param.12) | copy-start | bytes 2359300
  126.0 6.7 %copy-start.13 = (f32[512,768]{1,0:T(8,128)}, f32[512,768]{1,0:T(8,128)S(1)}, u32[]{:S(2)}) copy-start(f32[512,768]{1,0:T(8,128)S(1)} %get-tuple-element.65.normed_ref) | copy-start | bytes 4718596
  126.0 6.7 %copy-start.14 = (f32[512,3072]{1,0:T(8,128)}, f32[512,3072]{1,0:T(8,128)S(1)}, u32[]{:S(2)}) copy-start(f32[512,3072]{1,0:T(8,128)S(1)} %get-tuple-element.70.gp_ref) | copy-start | bytes 18874372
  126.0 6.7 %copy-start.36 = (bf16[768,512]{1,0:T(8,128)(2,1)}, bf16[768,512]{1,0:T(8,128)(2,1)S(1)}, u32[]{:S(2)}) copy-start(bf16[768,512]{1,0:T(8,128)(2,1)S(1)} %get-tuple-element.76.own_ref) | copy-start | bytes 2359300
  126.0 6.7 %copy-start.48 = (f32[512,1]{1,0:T(8,128)}, f32[512,1]{1,0:T(8,128)S(1)}, u32[]{:S(2)}) copy-start(f32[512,1]{1,0:T(8,128)S(1)} %get-tuple-element.69.inverse_ref) | copy-start | bytes 6148
  126.0 11.1 %collective-permute-start.8 = (bf16[512,3072]{1,0:T(8,128)(2,1)S(1)}, bf16[512,3072]{1,0:T(8,128)(2,1)S(1)}, u32[]{:S(2)}, u32[]{:S(2)}) collective-permute-start(bf16[512,3072]{1,0:T(8,128)(2,1)S(1)} %get-tuple-element.64.g_ref.own_ref), channel_id=1, source_target_pairs={{0,1},{1,0},{2,3},{3,2},{4,5},{5,4},{6,7},{7,6},{8,9},{9,8},{10,11... | collective-permute-start | bytes 9437192 | tf_op jit(solution)/shard_map/ppermute | solution.py:953
  135.4 1.7 collective-permute-start.9
  143.3 111.7 %reduce-scatter.5.cloned.1.call-start = ((), (), s32[]{:S(2)}) async-start(), calls=%async_computation.3 | async-start | bytes 737280 | tf_op jit(solution)/shard_map/reduce_scatter | solution.py:1197
  143.3 17.8 %copy-start.37 = (bf16[768,512]{1,0:T(8,128)(2,1)S(1)}, bf16[768,512]{1,0:T(8,128)(2,1)}, u32[]{:S(2)}) copy-start(bf16[768,512]{1,0:T(8,128)(2,1)} %copy-done.36) | copy-start | bytes 2359300
  160.8 9.1 %collective-permute-start.12 = (bf16[512,1536]{1,0:T(8,128)(2,1)}, bf16[512,1536]{1,0:T(8,128)(2,1)}, u32[]{:S(2)}, u32[]{:S(2)}) collective-permute-start(bf16[512,1536]{1,0:T(8,128)(2,1)} %get-tuple-element.78), channel_id=1, source_target_pairs={{0,1},{1,0},{2,3},{3,2},{4,5},{5,4},{6,7},{7,6},{8,9},{9,8},{10,11... | collective-permute-start | bytes 4718600 | tf_op jit(solution)/shard_map/ppermute | solution.py:953
  161.1 8.7 %collective-permute-start.11 = (bf16[768,512]{1,0:T(8,128)(2,1)S(1)}, bf16[768,512]{1,0:T(8,128)(2,1)}, u32[]{:S(2)}, u32[]{:S(2)}) collective-permute-start(bf16[768,512]{1,0:T(8,128)(2,1)S(1)} %copy-done.37), channel_id=1, source_target_pairs={{0,1},{1,0},{2,3},{3,2},{4,5},{5,4},{6,7},{7,6},{8,9},{9,8},{10,11... | collective-permute-start | bytes 2359304 | tf_op jit(solution)/shard_map/ppermute | solution.py:953
  161.4 4.8 %collective-permute-start.13 = (bf16[512,384]{1,0:T(8,128)(2,1)}, bf16[512,384]{1,0:T(8,128)(2,1)S(1)}, u32[]{:S(2)}, u32[]{:S(2)}) collective-permute-start(bf16[512,384]{1,0:T(8,128)(2,1)} %get-tuple-element.82), channel_id=1, source_target_pairs={{0,1},{1,0},{2,3},{3,2},{4,5},{5,4},{6,7},{7,6},{8,9},{9,8},{10,11... | collective-permute-start | bytes 1179656 | tf_op jit(solution)/shard_map/ppermute | solution.py:953
  161.6 15.4 %collective-permute-start.10 = (bf16[512,384]{1,0:T(8,128)(2,1)}, bf16[512,384]{1,0:T(8,128)(2,1)}, u32[]{:S(2)}, u32[]{:S(2)}) collective-permute-start(bf16[512,384]{1,0:T(8,128)(2,1)} %get-tuple-element.74), channel_id=1, source_target_pairs={{0,1},{1,0},{2,3},{3,2},{4,5},{5,4},{6,7},{7,6},{8,9},{9,8},{10,11... | collective-permute-start | bytes 1179656 | tf_op jit(solution)/shard_map/ppermute | solution.py:953
  174.4 34.0 %collective-permute-start.17 = (bf16[8,48,768]{2,1,0:T(8,128)(2,1)S(1)}, bf16[8,48,768]{2,1,0:T(8,128)(2,1)S(1)}, u32[]{:S(2)}, u32[]{:S(2)}) collective-permute-start(bf16[8,48,768]{2,1,0:T(8,128)(2,1)S(1)} %dynamic-slice_bitcast_fusion.1.refs_0_), channel_id=1, source_target_pairs={{0,2},{1,3},{2,0},{3,1},{4,6},{5,7},{6,4},{7,5},{8,10},{9,11},{10,... | collective-permute-start | bytes 1769480 | tf_op jit(solution)/shard_map/ppermute | solution.py:958
  176.0 33.3 %collective-permute-start.18 = (bf16[8,48,768]{2,1,0:T(8,128)(2,1)S(1)}, bf16[8,48,768]{2,1,0:T(8,128)(2,1)S(1)}, u32[]{:S(2)}, u32[]{:S(2)}) collective-permute-start(bf16[8,48,768]{2,1,0:T(8,128)(2,1)S(1)} %bitcast.81), channel_id=1, source_target_pairs={{0,4},{1,5},{2,6},{3,7},{4,0},{5,1},{6,2},{7,3},{8,12},{9,13},{10,... | collective-permute-start | bytes 1769480 | tf_op jit(solution)/shard_map/ppermute | solution.py:958
  177.0 24.1 %copy-start.4 = (bf16[768,1024]{1,0:T(8,128)(2,1)S(1)}, bf16[768,1024]{1,0:T(8,128)(2,1)}, u32[]{:S(2)}) copy-start(bf16[768,1024]{1,0:T(8,128)(2,1)} %get-tuple-element.113.refs_0_.turned_ref) | copy-start | bytes 4718596
  177.0 24.1 %copy-start.47 = (f32[768,128]{1,0:T(8,128)S(1)}, f32[768,128]{1,0:T(8,128)}, u32[]{:S(2)}) copy-start(f32[768,128]{1,0:T(8,128)} %get-tuple-element.89.widen_ref) | copy-start | bytes 1179652
  177.0 24.1 %copy-start.52 = (f32[8,768]{1,0:T(8,128)S(1)}, f32[8,768]{1,0:T(8,128)}, u32[]{:S(2)}) copy-start(f32[8,768]{1,0:T(8,128)} %copy-done.51) | copy-start | bytes 73732
  177.0 24.1 %copy-start.53 = (f32[8,768]{1,0:T(8,128)S(1)}, f32[8,768]{1,0:T(8,128)}, u32[]{:S(2)}) copy-start(f32[8,768]{1,0:T(8,128)} %get-tuple-element.87.first_ref) | copy-start | bytes 73732
  203.8 6.3 %copy-start.6 = (bf16[1024,1152]{1,0:T(8,128)(2,1)S(1)}, bf16[1024,1152]{1,0:T(8,128)(2,1)}, u32[]{:S(2)}) copy-start(bf16[1024,1152]{1,0:T(8,128)(2,1)} %copy-done.5) | copy-start | bytes 7077892
  205.9 18.7 %collective-permute-start.16 = (bf16[8,48,896]{2,1,0:T(8,128)(2,1)}, bf16[8,48,896]{2,1,0:T(8,128)(2,1)}, u32[]{:S(2)}, u32[]{:S(2)}) collective-permute-start(bf16[8,48,896]{2,1,0:T(8,128)(2,1)} %bitcast.24.refs_1_.refs_11_), channel_id=1, source_target_pairs={{0,4},{1,5},{2,6},{3,7},{4,0},{5,1},{6,2},{7,3},{8,12},{9,13},{10,... | collective-permute-start | bytes 2064392 | tf_op jit(solution)/shard_map/ppermute | solution.py:958
  207.8 16.0 %collective-permute-start.15 = (bf16[8,48,768]{2,1,0:T(8,128)(2,1)}, bf16[8,48,768]{2,1,0:T(8,128)(2,1)}, u32[]{:S(2)}, u32[]{:S(2)}) collective-permute-start(bf16[8,48,768]{2,1,0:T(8,128)(2,1)} %dynamic-slice_bitcast_fusion.refs_0_.refs_10_), channel_id=1, source_target_pairs={{0,2},{1,3},{2,0},{3,1},{4,6},{5,7},{6,4},{7,5},{8,10},{9,11},{10,... | collective-permute-start | bytes 1769480 | tf_op jit(solution)/shard_map/ppermute | solution.py:958
  218.3 13.7 %collective-permute-start.21 = (bf16[4,48,768]{2,1,0:T(8,128)(2,1)}, bf16[4,48,768]{2,1,0:T(8,128)(2,1)S(1)}, u32[]{:S(2)}, u32[]{:S(2)}) collective-permute-start(bf16[4,48,768]{2,1,0:T(8,128)(2,1)} %get-tuple-element.94.refs_8_), channel_id=1, source_target_pairs={{0,4},{1,5},{2,6},{3,7},{4,0},{5,1},{6,2},{7,3},{8,12},{9,13},{10,... | collective-permute-start | bytes 884744 | tf_op jit(solution)/shard_map/ppermute | solution.py:958
  219.8 12.2 %collective-permute-start.22 = (bf16[4,48,768]{2,1,0:T(8,128)(2,1)}, bf16[4,48,768]{2,1,0:T(8,128)(2,1)S(1)}, u32[]{:S(2)}, u32[]{:S(2)}) collective-permute-start(bf16[4,48,768]{2,1,0:T(8,128)(2,1)} %get-tuple-element.95.refs_9_), channel_id=1, source_target_pairs={{0,2},{1,3},{2,0},{3,1},{4,6},{5,7},{6,4},{7,5},{8,10},{9,11},{10,... | collective-permute-start | bytes 884744 | tf_op jit(solution)/shard_map/ppermute | solution.py:958
  230.2 7.9 %collective-permute-start.20 = (bf16[4,48,896]{2,1,0:T(8,128)(2,1)S(1)}, bf16[4,48,896]{2,1,0:T(8,128)(2,1)S(1)}, u32[]{:S(2)}, u32[]{:S(2)}) collective-permute-start(bf16[4,48,896]{2,1,0:T(8,128)(2,1)S(1)} %get-tuple-element.99.refs_9_), channel_id=1, source_target_pairs={{0,2},{1,3},{2,0},{3,1},{4,6},{5,7},{6,4},{7,5},{8,10},{9,11},{10,... | collective-permute-start | bytes 1032200 | tf_op jit(solution)/shard_map/ppermute | solution.py:958
  231.4 6.7 %collective-permute-start.19 = (bf16[4,48,768]{2,1,0:T(8,128)(2,1)S(1)}, bf16[4,48,768]{2,1,0:T(8,128)(2,1)S(1)}, u32[]{:S(2)}, u32[]{:S(2)}) collective-permute-start(bf16[4,48,768]{2,1,0:T(8,128)(2,1)S(1)} %get-tuple-element.97.refs_8_), channel_id=1, source_target_pairs={{0,4},{1,5},{2,6},{3,7},{4,0},{5,1},{6,2},{7,3},{8,12},{9,13},{10,... | collective-permute-start | bytes 884744 | tf_op jit(solution)/shard_map/ppermute | solution.py:958
  232.7 12.2 %collective-permute-start.24 = (bf16[2,48,1536]{2,1,0:T(8,128)(2,1)S(1)}, bf16[2,48,1536]{2,1,0:T(8,128)(2,1)S(1)}, u32[]{:S(2)}, u32[]{:S(2)}) collective-permute-start(bf16[2,48,1536]{2,1,0:T(8,128)(2,1)S(1)} %get-tuple-element.102.refs_8_), channel_id=1, source_target_pairs={{0,8},{1,9},{2,10},{3,11},{4,12},{5,13},{6,14},{7,15},{8,0},{9,1},... | collective-permute-start | bytes 884744 | tf_op jit(solution)/shard_map/ppermute | solution.py:958
  238.8 14.9 %collective-permute-start.23 = (bf16[2,48,1664]{2,1,0:T(8,128)(2,1)S(1)}, bf16[2,48,1664]{2,1,0:T(8,128)(2,1)S(1)}, u32[]{:S(2)}, u32[]{:S(2)}) collective-permute-start(bf16[2,48,1664]{2,1,0:T(8,128)(2,1)S(1)} %get-tuple-element.104.refs_4_), channel_id=1, source_target_pairs={{0,8},{1,9},{2,10},{3,11},{4,12},{5,13},{6,14},{7,15},{8,0},{9,1},... | collective-permute-start | bytes 958472 | tf_op jit(solution)/shard_map/ppermute | solution.py:958
  245.5 9.4 %collective-permute-start.27 = (bf16[1,48,1536]{2,1,0:T(8,128)(2,1)S(1)}, bf16[1,48,1536]{2,1,0:T(8,128)(2,1)S(1)}, u32[]{:S(2)}, u32[]{:S(2)}) collective-permute-start(bf16[1,48,1536]{2,1,0:T(8,128)(2,1)S(1)} %get-tuple-element.106.refs_4_), channel_id=1, source_target_pairs={{0,16},{1,17},{2,18},{3,19},{4,20},{5,21},{6,22},{7,23},{8,24},{9,... | collective-permute-start | bytes 442376 | tf_op jit(solution)/shard_map/ppermute | solution.py:958
  254.3 9.1 %collective-permute-start.25 = (bf16[1,48,1664]{2,1,0:T(8,128)(2,1)S(1)}, bf16[1,48,1664]{2,1,0:T(8,128)(2,1)}, u32[]{:S(2)}, u32[]{:S(2)}) collective-permute-start(bf16[1,48,1664]{2,1,0:T(8,128)(2,1)S(1)} %get-tuple-element.108), channel_id=1, source_target_pairs={{0,16},{1,17},{2,18},{3,19},{4,20},{5,21},{6,22},{7,23},{8,24},{9,... | collective-permute-start | bytes 479240 | tf_op jit(solution)/shard_map/ppermute | solution.py:958
  254.9 9.6 %collective-permute-start.28 = (f32[48,1536]{1,0:T(8,128)S(1)}, f32[48,1536]{1,0:T(8,128)S(1)}, u32[]{:S(2)}, u32[]{:S(2)}) collective-permute-start(f32[48,1536]{1,0:T(8,128)S(1)} %add_bitcast_fusion.1), channel_id=1, source_target_pairs={{0,1},{1,0},{2,3},{3,2},{4,5},{5,4},{6,7},{7,6},{8,9},{9,8},{10,11... | collective-permute-start | bytes 884744 | tf_op jit(solution)/shard_map/ppermute | solution.py:953
  262.8 4.6 %collective-permute-start.14 = (f32[512,768]{1,0:T(8,128)S(1)}, f32[512,768]{1,0:T(8,128)S(1)}, u32[]{:S(2)}, u32[]{:S(2)}) collective-permute-start(f32[512,768]{1,0:T(8,128)S(1)} %get-tuple-element.93), channel_id=1, source_target_pairs={{0,1},{1,0},{2,3},{3,2},{4,5},{5,4},{6,7},{7,6},{8,9},{9,8},{10,11... | collective-permute-start | bytes 4718600 | tf_op jit(solution)/shard_map/ppermute | solution.py:953
  264.3 3.3 %collective-permute-start.26 = (f32[48,1664]{1,0:T(8,128)S(1)}, f32[48,1664]{1,0:T(8,128)S(1)}, u32[]{:S(2)}, u32[]{:S(2)}) collective-permute-start(f32[48,1664]{1,0:T(8,128)S(1)} %add_bitcast_fusion.own_ref), channel_id=1, source_target_pairs={{0,1},{1,0},{2,3},{3,2},{4,5},{5,4},{6,7},{7,6},{8,9},{9,8},{10,11... | collective-permute-start | bytes 958472 | tf_op jit(solution)/shard_map/ppermute | solution.py:953
  264.5 2.8 collective-permute-start.29
  (43 other events, 75.8 us)
Sparse Core Ops, SparseCore 0:
  11.5 99.5 all-gather.1
  143.4 36.3 reduce-scatter.6
  220.9 22.7 reduce-scatter.4
